TPU v7x, 256 devices: a whole 4x4x8 slice. The times are simulated.
256 devices in a mesh: tile: 64 (over z, x, y_hi), head: 4 (over y_lo, core).
Axes of the slice: x: 4, y: 4 (y_hi: 2, y_lo: 2; y = y_hi * 2 + y_lo), z: 8, core: 2. Of those that a mesh axis runs over, the one named last changes fastest.
Arguments:
- queries: bfloat16 [10240, 3072], P('tile', 'head'), as said below
- keys: bfloat16 [10240, 3072], P('tile', 'head'), as said below
- values: bfloat16 [10240, 3072], P('tile', 'head'), may hold values from -5 to 5
- w_out: bfloat16 [3072, 3072], P(None, 'head'), may hold values from -0.109375 to 0.109375
- out_grad: bfloat16 [10240, 3072], P('tile', 'head'), may hold values from -5 to 5
- tile_valid: int32 [64], replicated, may hold values 0 or 1
Outputs:
- mixed: bfloat16 [10240, 3072], P('tile', 'head')
- query_grad: bfloat16 [10240, 3072], P('tile', 'head')
- key_grad: bfloat16 [10240, 3072], P('tile', 'head')
- value_grad: bfloat16 [10240, 3072], P('tile', 'head')
Inputs may be any that keep to these rules, and one draw needn't show every extreme that they name: `queries`: entries lie within -5 to 5. `keys`: entries lie within -5 to 5.
All inputs are finite; a program needn't handle non-finite values.
Results may differ from a plain program's by a relative error of at most 0.012.
Values may be sent and summed in bfloat16 or wider, within the bound.
A program may use at most 64 MiB of HBM per device.

v0:
```python
import jax
import jax.numpy as jnp
from jax import lax
from jax.sharding import PartitionSpec as P

HD = 128
GT = 4


def passed_along(value, axis, steps):
    count = lax.axis_size(axis)
    leading, last = (max(0, -steps), min(count, count - steps))
    return lax.ppermute(value, axis, [(source, source + steps) for source in range(leading, last)])


def tile_flags(tile_time, tile_height, grid_height, tile_valid):
    tile_ids = jnp.arange(tile_valid.shape[0], dtype=jnp.int32)
    flags = []
    for step_time in (-1, 0, 1):
        for step_row in (-1, 0, 1):
            near_time = tile_time + step_time
            near_height = tile_height + step_row
            inside = (
                (near_time >= 0)
                & (near_time < GT)
                & (near_height >= 0)
                & (near_height < grid_height)
            )
            marked = (
                jnp.sum(jnp.where(tile_ids == near_time * grid_height + near_height, tile_valid, 0))
                > 0
            )
            flags.append(inside & (marked | (step_time == 0 and step_row == 0)))
    return jnp.stack(flags)


def on_device(queries, keys, values, w_out, out_grad, tile_valid):
    tile_tokens, feature_count = queries.shape
    head_count = feature_count // HD
    grid_height = lax.axis_size("tile") // GT
    tile_index = lax.axis_index("tile")
    tile_time = tile_index // grid_height
    tile_height = tile_index % grid_height
    score_scale = HD ** (-0.5)
    offsets = [(step_time, step_row) for step_time in (-1, 0, 1) for step_row in (-1, 0, 1)]
    attn_grad = jnp.dot(
        lax.all_gather(out_grad, "head", axis=1, tiled=True),
        w_out,
        preferred_element_type=jnp.float32,
    ).astype(jnp.bfloat16)
    paired = jnp.stack([keys, values])
    slots = []
    for step_time, step_row in offsets:
        if step_time == 0 and step_row == 0:
            slots.append(paired)
        else:
            slots.append(passed_along(paired, "tile", -(step_time * grid_height + step_row)))
    nearby = jnp.stack(slots)
    near_keys = nearby[:, 0].reshape(9 * tile_tokens, feature_count)
    near_values = nearby[:, 1].reshape(9 * tile_tokens, feature_count)
    key_flags = tile_flags(tile_time, tile_height, grid_height, tile_valid)
    allowed = jnp.repeat(key_flags, tile_tokens)[None, :]

    def forward_head(offset):
        query_head = lax.dynamic_slice_in_dim(queries, offset, HD, 1)
        key_head = lax.dynamic_slice_in_dim(near_keys, offset, HD, 1)
        value_head = lax.dynamic_slice_in_dim(near_values, offset, HD, 1)
        grad_head = lax.dynamic_slice_in_dim(attn_grad, offset, HD, 1)
        scores = (
            jnp.einsum("qd,kd->qk", query_head, key_head, preferred_element_type=jnp.float32)
            * score_scale
        )
        scores = jnp.where(allowed, scores, -jnp.inf)
        largest = jnp.max(scores, axis=1, keepdims=True)
        exponent = jnp.exp(scores - largest)
        total = jnp.sum(exponent, axis=1, keepdims=True)
        weights = (exponent / total).astype(jnp.bfloat16)
        attended_head = jnp.dot(weights, value_head, preferred_element_type=jnp.float32).astype(
            jnp.bfloat16
        )
        row_dot = jnp.sum(
            grad_head.astype(jnp.float32) * attended_head.astype(jnp.float32), axis=1, keepdims=True
        )
        weight_grad = jnp.einsum(
            "qd,kd->qk", grad_head, value_head, preferred_element_type=jnp.float32
        )
        score_grad = (weights.astype(jnp.float32) * (weight_grad - row_dot) * score_scale).astype(
            jnp.bfloat16
        )
        query_part = jnp.dot(score_grad, key_head, preferred_element_type=jnp.float32).astype(
            jnp.bfloat16
        )
        return (
            attended_head,
            query_part,
            weights,
            score_grad,
            query_head,
            grad_head,
            largest,
            total,
            row_dot,
        )

    zero_tokens = jnp.zeros((tile_tokens, feature_count), jnp.bfloat16)

    def head_step(head, carry):
        attended, query_grad, key_parts, value_parts = carry
        offset = head * HD
        (
            attended_head,
            query_part,
            weights,
            score_grad,
            query_head,
            grad_head,
            largest,
            total,
            row_dot,
        ) = forward_head(offset)
        key_part = jnp.einsum(
            "qk,qd->kd", score_grad, query_head, preferred_element_type=jnp.float32
        )
        value_part = jnp.einsum("qk,qd->kd", weights, grad_head, preferred_element_type=jnp.float32)
        attended = lax.dynamic_update_slice_in_dim(attended, attended_head, offset, 1)
        query_grad = lax.dynamic_update_slice_in_dim(query_grad, query_part, offset, 1)
        key_parts = lax.dynamic_update_slice_in_dim(key_parts, key_part, offset, 1)
        value_parts = lax.dynamic_update_slice_in_dim(value_parts, value_part, offset, 1)
        return (attended, query_grad, key_parts, value_parts)

    start_state = (
        zero_tokens,
        zero_tokens,
        jnp.zeros((9 * tile_tokens, feature_count), jnp.float32),
        jnp.zeros((9 * tile_tokens, feature_count), jnp.float32),
    )
    attended, query_grad, key_parts, value_parts = lax.fori_loop(
        0, head_count, head_step, start_state
    )
    grad_parts = jnp.stack(
        [
            key_parts.reshape(9, tile_tokens, feature_count),
            value_parts.reshape(9, tile_tokens, feature_count),
        ],
        axis=1,
    )
    owned = grad_parts[4]
    for slot, (step_time, step_row) in enumerate(offsets):
        if not (step_time == 0 and step_row == 0):
            owned = owned + passed_along(
                grad_parts[slot], "tile", step_time * grid_height + step_row
            )
    key_grad = owned[0].astype(jnp.bfloat16)
    value_grad = owned[1].astype(jnp.bfloat16)
    projected = jnp.einsum("qf,df->qd", attended, w_out, preferred_element_type=jnp.float32)
    mixed = lax.psum_scatter(projected, "head", scatter_dimension=1, tiled=True).astype(
        jnp.bfloat16
    )
    return (mixed, query_grad, key_grad, value_grad)


def solution(mesh):
    return jax.shard_map(
        on_device,
        mesh=mesh,
        in_specs=(
            P("tile", "head"),
            P("tile", "head"),
            P("tile", "head"),
            P(None, "head"),
            P("tile", "head"),
            P(),
        ),
        out_specs=(P("tile", "head"), P("tile", "head"), P("tile", "head"), P("tile", "head")),
        check_vma=False,
    )
```

profile of v0, /device:TPU:183, one launch (start us, length us, event | category | flops | bytes accessed | tf_op | source)
XLA Modules:
  0.0 433.2 jit_solution(17929537260463000536)
XLA Ops:
  8.3 2.2 collective-permute-start.6
  10.5 2.1 collective-permute-start.5
  12.6 4.5 %collective-permute-start.4 = (bf16[2,160,768]{2,1,0:T(8,128)(2,1)S(1)}, bf16[2,160,768]{2,1,0:T(8,128)(2,1)}, u32[]{:S(2)}, u32[]{:S(2)}) collective-permute-start(bf16[2,160,768]{2,1,0:T(8,128)(2,1)S(1)} %pad_maximum_fusion.1), channel_id=1, source_target_pairs={{4,0},{8,4},{12,8},{16,12},{20,16},{24,20},{28,24},{32,28},{36,32}... | collective-permute-start | bytes 1474568 | tf_op jit(solution)/shard_map/ppermute | solution.py:13
  17.0 5.0 %collective-permute-start.1 = (bf16[2,160,768]{2,1,0:T(8,128)(2,1)S(1)}, bf16[2,160,768]{2,1,0:T(8,128)(2,1)}, u32[]{:S(2)}, u32[]{:S(2)}) collective-permute-start(bf16[2,160,768]{2,1,0:T(8,128)(2,1)S(1)} %pad_maximum_fusion.1), channel_id=1, source_target_pairs={{0,64},{4,68},{8,72},{12,76},{16,80},{20,84},{24,88},{28,92},{32,9... | collective-permute-start | bytes 1474568 | tf_op jit(solution)/shard_map/ppermute | solution.py:13
  23.5 23.3 %all_gather.3 = bf16[160,3072]{1,0:T(8,128)(2,1)S(1)} all-gather(bf16[160,768]{1,0:T(8,128)(2,1)} %param.12), channel_id=1, replica_groups=mesh['tile'=64,'head'=4] {'head'}, dimensions={1}, use_global_device_ids=true | all-gather | bytes 1228800 | tf_op jit(solution)/shard_map/all_gather | solution.py:47
  46.7 1.4 fusion.55
  53.3 3.3 convolution_convert_fusion.2
  56.6 18.0 %collective-permute-done = bf16[2,160,768]{2,1,0:T(8,128)(2,1)} collective-permute-done((bf16[2,160,768]{2,1,0:T(8,128)(2,1)S(1)}, bf16[2,160,768]{2,1,0:T(8,128)(2,1)}, u32[]{:S(2)}, u32[]{:S(2)}) %collective-permute-start) | collective-permute-done | bytes 491552 | tf_op jit(solution)/shard_map/ppermute | solution.py:13
  74.6 1.9 collective-permute-start.2
  77.6 1.9 collective-permute-start.3
  80.6 15.4 %collective-permute-done.2 = bf16[2,160,768]{2,1,0:T(8,128)(2,1)S(1)} collective-permute-done((bf16[2,160,768]{2,1,0:T(8,128)(2,1)S(1)}, bf16[2,160,768]{2,1,0:T(8,128)(2,1)S(1)}, u32[]{:S(2)}, u32[]{:S(2)}) %collective-permute-start.2) | collective-permute-done | bytes 491552 | tf_op jit(solution)/shard_map/ppermute | solution.py:13
  96.0 2.8 collective-permute-start.7
  98.9 7.7 %collective-permute-done.3 = bf16[2,160,768]{2,1,0:T(8,128)(2,1)S(1)} collective-permute-done((bf16[2,160,768]{2,1,0:T(8,128)(2,1)S(1)}, bf16[2,160,768]{2,1,0:T(8,128)(2,1)S(1)}, u32[]{:S(2)}, u32[]{:S(2)}) %collective-permute-start.3) | collective-permute-done | bytes 491552 | tf_op jit(solution)/shard_map/ppermute | solution.py:13
  107.9 1.7 fusion.57
  109.7 2.4 broadcast.15.clone
  112.0 2.3 broadcast.15
  114.3 46.2 %while.20 = (s32[]{:T(128)}, bf16[160,768]{1,0:T(8,128)(2,1)S(1)}, bf16[160,768]{1,0:T(8,128)(2,1)S(1)}, f32[1440,768]{1,0:T(8,128)}, f32[1440,768]{1,0:T(8,128)...) while((s32[]{:T(128)}, bf16[160,768]{1,0:T(8,128)(2,1)S(1)}, ...), condition=%wide.region_12.13_spmd.clone, body=%wide.region_8.12_spmd.clone.sunk | while | flops 357012000 | bytes 9448000 | solution.py:137
  114.5 1.4 fusion.89
  118.5 2.1 convolution_dynamic-update-slice_fusion.4
  120.7 1.4 convolution_dynamic-update-slice_fusion.5
  122.3 1.4 fusion.89
  126.3 2.1 convolution_dynamic-update-slice_fusion.4
  129.9 1.4 fusion.89
  134.0 2.1 convolution_dynamic-update-slice_fusion.4
  136.1 1.4 convolution_dynamic-update-slice_fusion.5
  137.6 1.4 fusion.89
  141.6 2.2 convolution_dynamic-update-slice_fusion.4
  143.8 1.4 convolution_dynamic-update-slice_fusion.5
  145.4 1.4 fusion.89
  149.4 2.1 convolution_dynamic-update-slice_fusion.4
  153.0 1.4 fusion.89
  157.0 2.2 convolution_dynamic-update-slice_fusion.4
  159.2 1.4 convolution_dynamic-update-slice_fusion.5
  160.6 5.4 %fusion.58 = f32[160,3072]{1,0:T(8,128)} fusion(bf16[160,768]{1,0:T(8,128)(2,1)S(1)} %get-tuple-element.176, bf16[3072,768]{1,0:T(8,128)(2,1)} %param.11), kind=kOutput, calls=%fused_computation.105 | convolution fusion | flops 754974720 | bytes 6930432 | tf_op jit(solution)/shard_map/qf,df->qd/dot_general | solution.py:155
  166.1 3.9 fusion.35
  170.0 8.1 %collective-permute-start.8 = (f32[2,160,768]{2,1,0:T(8,128)S(1)}, f32[2,160,768]{2,1,0:T(8,128)S(1)}, u32[]{:S(2)}, u32[]{:S(2)}) collective-permute-start(f32[2,160,768]{2,1,0:T(8,128)S(1)} %get-tuple-element.235), channel_id=1, source_target_pairs={{68,0},{72,4},{76,8},{80,12},{84,16},{88,20},{92,24},{96,28},{100,... | collective-permute-start | bytes 2949128 | tf_op jit(solution)/shard_map/ppermute | solution.py:13
  178.1 15.2 %collective-permute-start.9 = (f32[2,160,768]{2,1,0:T(8,128)S(1)}, f32[2,160,768]{2,1,0:T(8,128)S(1)}, u32[]{:S(2)}, u32[]{:S(2)}) collective-permute-start(f32[2,160,768]{2,1,0:T(8,128)S(1)} %get-tuple-element.236), channel_id=1, source_target_pairs={{64,0},{68,4},{72,8},{76,12},{80,16},{84,20},{88,24},{92,28},{96,3... | collective-permute-start | bytes 2949128 | tf_op jit(solution)/shard_map/ppermute | solution.py:13
  193.3 1.9 collective-permute-start.10
  195.2 4.6 %collective-permute-start.11 = (f32[2,160,768]{2,1,0:T(8,128)S(1)}, f32[2,160,768]{2,1,0:T(8,128)S(1)}, u32[]{:S(2)}, u32[]{:S(2)}) collective-permute-start(f32[2,160,768]{2,1,0:T(8,128)S(1)} %get-tuple-element.238), channel_id=1, source_target_pairs={{4,0},{8,4},{12,8},{16,12},{20,16},{24,20},{28,24},{32,28},{36,32}... | collective-permute-start | bytes 2949128 | tf_op jit(solution)/shard_map/ppermute | solution.py:13
  199.8 5.2 %collective-permute-start.12 = (f32[2,160,768]{2,1,0:T(8,128)S(1)}, f32[2,160,768]{2,1,0:T(8,128)S(1)}, u32[]{:S(2)}, u32[]{:S(2)}) collective-permute-start(f32[2,160,768]{2,1,0:T(8,128)S(1)} %get-tuple-element.239), channel_id=1, source_target_pairs={{0,4},{4,8},{8,12},{12,16},{16,20},{20,24},{24,28},{28,32},{32,36}... | collective-permute-start | bytes 2949128 | tf_op jit(solution)/shard_map/ppermute | solution.py:13
  205.1 4.5 %collective-permute-start.13 = (f32[2,160,768]{2,1,0:T(8,128)S(1)}, f32[2,160,768]{2,1,0:T(8,128)S(1)}, u32[]{:S(2)}, u32[]{:S(2)}) collective-permute-start(f32[2,160,768]{2,1,0:T(8,128)S(1)} %get-tuple-element.240), channel_id=1, source_target_pairs={{0,60},{4,64},{8,68},{12,72},{16,76},{20,80},{24,84},{28,88},{32,9... | collective-permute-start | bytes 2949128 | tf_op jit(solution)/shard_map/ppermute | solution.py:13
  209.5 12.6 %collective-permute-done.9 = f32[2,160,768]{2,1,0:T(8,128)S(1)} collective-permute-done((f32[2,160,768]{2,1,0:T(8,128)S(1)}, f32[2,160,768]{2,1,0:T(8,128)S(1)}, u32[]{:S(2)}, u32[]{:S(2)}) %collective-permute-start.9) | collective-permute-done | bytes 983072 | tf_op jit(solution)/shard_map/ppermute | solution.py:13
  223.5 57.5 %collective-permute-done.10 = f32[2,160,768]{2,1,0:T(8,128)S(1)} collective-permute-done((f32[2,160,768]{2,1,0:T(8,128)S(1)}, f32[2,160,768]{2,1,0:T(8,128)S(1)}, u32[]{:S(2)}, u32[]{:S(2)}) %collective-permute-start.10) | collective-permute-done | bytes 983072 | tf_op jit(solution)/shard_map/ppermute | solution.py:13
  280.9 1.9 collective-permute-start.14
  282.8 82.0 %collective-permute-done.11 = f32[2,160,768]{2,1,0:T(8,128)S(1)} collective-permute-done((f32[2,160,768]{2,1,0:T(8,128)S(1)}, f32[2,160,768]{2,1,0:T(8,128)S(1)}, u32[]{:S(2)}, u32[]{:S(2)}) %collective-permute-start.11) | collective-permute-done | bytes 983072 | tf_op jit(solution)/shard_map/ppermute | solution.py:13
  364.9 57.4 %collective-permute-done.14 = f32[2,160,768]{2,1,0:T(8,128)S(1)} collective-permute-done((f32[2,160,768]{2,1,0:T(8,128)S(1)}, f32[2,160,768]{2,1,0:T(8,128)S(1)}, u32[]{:S(2)}, u32[]{:S(2)}) %collective-permute-start.14) | collective-permute-done | bytes 983072 | tf_op jit(solution)/shard_map/ppermute | solution.py:13
  422.2 1.5 fusion.47
  424.6 1.7 convert_element_type.64
  (89 shorter events, 27.5 us)
Async XLA Ops:
  7.2 417.4 %reduce-scatter.2.cloned.1.call-start = ((), (), s32[]{:S(2)}) async-start(), calls=%async_computation.1 | async-start | bytes 2457600 | tf_op jit(solution)/shard_map/reduce_scatter | solution.py:156
  8.3 99.5 %collective-permute-start.6 = (bf16[2,160,768]{2,1,0:T(8,128)(2,1)S(1)}, bf16[2,160,768]{2,1,0:T(8,128)(2,1)S(1)}, u32[]{:S(2)}, u32[]{:S(2)}) collective-permute-start(bf16[2,160,768]{2,1,0:T(8,128)(2,1)S(1)} %pad_maximum_fusion.1), channel_id=1, source_target_pairs={{64,0},{68,4},{72,8},{76,12},{80,16},{84,20},{88,24},{92,28},{96,3... | collective-permute-start | bytes 1474568 | tf_op jit(solution)/shard_map/ppermute | solution.py:13
  10.5 97.2 %collective-permute-start.5 = (bf16[2,160,768]{2,1,0:T(8,128)(2,1)S(1)}, bf16[2,160,768]{2,1,0:T(8,128)(2,1)S(1)}, u32[]{:S(2)}, u32[]{:S(2)}) collective-permute-start(bf16[2,160,768]{2,1,0:T(8,128)(2,1)S(1)} %pad_maximum_fusion.1), channel_id=1, source_target_pairs={{60,0},{64,4},{68,8},{72,12},{76,16},{80,20},{84,24},{88,28},{92,3... | collective-permute-start | bytes 1474568 | tf_op jit(solution)/shard_map/ppermute | solution.py:13
  12.6 94.1 %collective-permute-start.4 = (bf16[2,160,768]{2,1,0:T(8,128)(2,1)S(1)}, bf16[2,160,768]{2,1,0:T(8,128)(2,1)}, u32[]{:S(2)}, u32[]{:S(2)}) collective-permute-start(bf16[2,160,768]{2,1,0:T(8,128)(2,1)S(1)} %pad_maximum_fusion.1), channel_id=1, source_target_pairs={{4,0},{8,4},{12,8},{16,12},{20,16},{24,20},{28,24},{32,28},{36,32}... | collective-permute-start | bytes 1474568 | tf_op jit(solution)/shard_map/ppermute | solution.py:13
  17.0 60.6 %collective-permute-start.1 = (bf16[2,160,768]{2,1,0:T(8,128)(2,1)S(1)}, bf16[2,160,768]{2,1,0:T(8,128)(2,1)}, u32[]{:S(2)}, u32[]{:S(2)}) collective-permute-start(bf16[2,160,768]{2,1,0:T(8,128)(2,1)S(1)} %pad_maximum_fusion.1), channel_id=1, source_target_pairs={{0,64},{4,68},{8,72},{12,76},{16,80},{20,84},{24,88},{28,92},{32,9... | collective-permute-start | bytes 1474568 | tf_op jit(solution)/shard_map/ppermute | solution.py:13
  22.1 52.5 %collective-permute-start = (bf16[2,160,768]{2,1,0:T(8,128)(2,1)S(1)}, bf16[2,160,768]{2,1,0:T(8,128)(2,1)}, u32[]{:S(2)}, u32[]{:S(2)}) collective-permute-start(bf16[2,160,768]{2,1,0:T(8,128)(2,1)S(1)} %pad_maximum_fusion.1), channel_id=1, source_target_pairs={{0,68},{4,72},{8,76},{12,80},{16,84},{20,88},{24,92},{28,96},{32,1... | collective-permute-start | bytes 1474568 | tf_op jit(solution)/shard_map/ppermute | solution.py:13
  53.3 53.3 %copy-start = (bf16[160,768]{1,0:T(8,128)(2,1)S(1)}, bf16[160,768]{1,0:T(8,128)(2,1)}, u32[]{:S(2)}) copy-start(bf16[160,768]{1,0:T(8,128)(2,1)} %param.10) | copy-start | bytes 737284
  53.3 53.3 %copy-start.1 = (bf16[160,768]{1,0:T(8,128)(2,1)S(1)}, bf16[160,768]{1,0:T(8,128)(2,1)}, u32[]{:S(2)}) copy-start(bf16[160,768]{1,0:T(8,128)(2,1)} %param.9) | copy-start | bytes 737284
  74.6 21.4 %collective-permute-start.2 = (bf16[2,160,768]{2,1,0:T(8,128)(2,1)S(1)}, bf16[2,160,768]{2,1,0:T(8,128)(2,1)S(1)}, u32[]{:S(2)}, u32[]{:S(2)}) collective-permute-start(bf16[2,160,768]{2,1,0:T(8,128)(2,1)S(1)} %pad_maximum_fusion.1), channel_id=1, source_target_pairs={{0,60},{4,64},{8,68},{12,72},{16,76},{20,80},{24,84},{28,88},{32,9... | collective-permute-start | bytes 1474568 | tf_op jit(solution)/shard_map/ppermute | solution.py:13
  77.6 28.9 %collective-permute-start.3 = (bf16[2,160,768]{2,1,0:T(8,128)(2,1)S(1)}, bf16[2,160,768]{2,1,0:T(8,128)(2,1)S(1)}, u32[]{:S(2)}, u32[]{:S(2)}) collective-permute-start(bf16[2,160,768]{2,1,0:T(8,128)(2,1)S(1)} %pad_maximum_fusion.1), channel_id=1, source_target_pairs={{0,4},{4,8},{8,12},{12,16},{16,20},{20,24},{24,28},{28,32},{32,36}... | collective-permute-start | bytes 1474568 | tf_op jit(solution)/shard_map/ppermute | solution.py:13
  96.0 11.8 %collective-permute-start.7 = (bf16[2,160,768]{2,1,0:T(8,128)(2,1)S(1)}, bf16[2,160,768]{2,1,0:T(8,128)(2,1)S(1)}, u32[]{:S(2)}, u32[]{:S(2)}) collective-permute-start(bf16[2,160,768]{2,1,0:T(8,128)(2,1)S(1)} %pad_maximum_fusion.1), channel_id=1, source_target_pairs={{68,0},{72,4},{76,8},{80,12},{84,16},{88,20},{92,24},{96,28},{100,... | collective-permute-start | bytes 1474568 | tf_op jit(solution)/shard_map/ppermute | solution.py:13
  160.6 5.5 %copy-start.2 = (bf16[160,768]{1,0:T(8,128)(2,1)}, bf16[160,768]{1,0:T(8,128)(2,1)S(1)}, u32[]{:S(2)}) copy-start(bf16[160,768]{1,0:T(8,128)(2,1)S(1)} %get-tuple-element.173) | copy-start | bytes 737284
  166.0 256.2 %slice-start = ((s8[4423680]{0:T(1024)(128)(4,1)}), s8[229376]{0:T(1024)(128)(4,1)S(1)}, s32[]{:S(2)}) async-start(s8[4423680]{0:T(1024)(128)(4,1)} %bitcast.90), calls=%async_computation.2 | async-start | bytes 458752
  166.1 256.2 %slice-start.1 = ((s8[4423680]{0:T(1024)(128)(4,1)}), s8[4194304]{0:T(1024)(128)(4,1)S(1)}, s32[]{:S(2)}) async-start(s8[4423680]{0:T(1024)(128)(4,1)} %bitcast.90), calls=%async_computation.3 | async-start | bytes 8388608
  170.0 35.0 %collective-permute-start.8 = (f32[2,160,768]{2,1,0:T(8,128)S(1)}, f32[2,160,768]{2,1,0:T(8,128)S(1)}, u32[]{:S(2)}, u32[]{:S(2)}) collective-permute-start(f32[2,160,768]{2,1,0:T(8,128)S(1)} %get-tuple-element.235), channel_id=1, source_target_pairs={{68,0},{72,4},{76,8},{80,12},{84,16},{88,20},{92,24},{96,28},{100,... | collective-permute-start | bytes 2949128 | tf_op jit(solution)/shard_map/ppermute | solution.py:13
  178.1 44.0 %collective-permute-start.9 = (f32[2,160,768]{2,1,0:T(8,128)S(1)}, f32[2,160,768]{2,1,0:T(8,128)S(1)}, u32[]{:S(2)}, u32[]{:S(2)}) collective-permute-start(f32[2,160,768]{2,1,0:T(8,128)S(1)} %get-tuple-element.236), channel_id=1, source_target_pairs={{64,0},{68,4},{72,8},{76,12},{80,16},{84,20},{88,24},{92,28},{96,3... | collective-permute-start | bytes 2949128 | tf_op jit(solution)/shard_map/ppermute | solution.py:13
  193.3 87.6 %collective-permute-start.10 = (f32[2,160,768]{2,1,0:T(8,128)S(1)}, f32[2,160,768]{2,1,0:T(8,128)S(1)}, u32[]{:S(2)}, u32[]{:S(2)}) collective-permute-start(f32[2,160,768]{2,1,0:T(8,128)S(1)} %get-tuple-element.237), channel_id=1, source_target_pairs={{60,0},{64,4},{68,8},{72,12},{76,16},{80,20},{84,24},{88,28},{92,3... | collective-permute-start | bytes 2949128 | tf_op jit(solution)/shard_map/ppermute | solution.py:13
  195.2 169.6 %collective-permute-start.11 = (f32[2,160,768]{2,1,0:T(8,128)S(1)}, f32[2,160,768]{2,1,0:T(8,128)S(1)}, u32[]{:S(2)}, u32[]{:S(2)}) collective-permute-start(f32[2,160,768]{2,1,0:T(8,128)S(1)} %get-tuple-element.238), channel_id=1, source_target_pairs={{4,0},{8,4},{12,8},{16,12},{20,16},{24,20},{28,24},{32,28},{36,32}... | collective-permute-start | bytes 2949128 | tf_op jit(solution)/shard_map/ppermute | solution.py:13
  199.8 165.0 %collective-permute-start.12 = (f32[2,160,768]{2,1,0:T(8,128)S(1)}, f32[2,160,768]{2,1,0:T(8,128)S(1)}, u32[]{:S(2)}, u32[]{:S(2)}) collective-permute-start(f32[2,160,768]{2,1,0:T(8,128)S(1)} %get-tuple-element.239), channel_id=1, source_target_pairs={{0,4},{4,8},{8,12},{12,16},{16,20},{20,24},{24,28},{28,32},{32,36}... | collective-permute-start | bytes 2949128 | tf_op jit(solution)/shard_map/ppermute | solution.py:13
  205.1 159.8 %collective-permute-start.13 = (f32[2,160,768]{2,1,0:T(8,128)S(1)}, f32[2,160,768]{2,1,0:T(8,128)S(1)}, u32[]{:S(2)}, u32[]{:S(2)}) collective-permute-start(f32[2,160,768]{2,1,0:T(8,128)S(1)} %get-tuple-element.240), channel_id=1, source_target_pairs={{0,60},{4,64},{8,68},{12,72},{16,76},{20,80},{24,84},{28,88},{32,9... | collective-permute-start | bytes 2949128 | tf_op jit(solution)/shard_map/ppermute | solution.py:13
  222.2 142.7 %collective-permute-start.15 = (f32[2,160,768]{2,1,0:T(8,128)S(1)}, f32[2,160,768]{2,1,0:T(8,128)S(1)}, u32[]{:S(2)}, u32[]{:S(2)}) collective-permute-start(f32[2,160,768]{2,1,0:T(8,128)S(1)} %get-tuple-element.241), channel_id=1, source_target_pairs={{0,68},{4,72},{8,76},{12,80},{16,84},{20,88},{24,92},{28,96},{32,1... | collective-permute-start | bytes 2949128 | tf_op jit(solution)/shard_map/ppermute | solution.py:13
  280.9 141.3 %collective-permute-start.14 = (f32[2,160,768]{2,1,0:T(8,128)S(1)}, f32[2,160,768]{2,1,0:T(8,128)S(1)}, u32[]{:S(2)}, u32[]{:S(2)}) collective-permute-start(f32[2,160,768]{2,1,0:T(8,128)S(1)} %get-tuple-element.242), channel_id=1, source_target_pairs={{0,64},{4,68},{8,72},{12,76},{16,80},{20,84},{24,88},{28,92},{32,9... | collective-permute-start | bytes 2949128 | tf_op jit(solution)/shard_map/ppermute | solution.py:13
Sparse Core Ops, SparseCore 0:
  166.2 170.6 reduce-scatter.1
where the time goes:
time: 435 us; the launch traced here: 433 us
  waiting for transfers between devices  251 us (58%)
  starting transfers between devices  64.4 us (15%)
  matrix products  49.7 us (11%)
  blocking collectives  23.3 us (5%)
  between operations  19.4 us (4%)
  other arithmetic  13.9 us (3%)
  local copies, waits for them, and re-layouts  11.7 us (3%)
    ppermute x16, waiting for transfers between devices, passed_along(): lax.ppermute(value, axis, [(source, source + steps) for source in range(l...  251 us
    ppermute x16, starting transfers between devices, passed_along(): lax.ppermute(value, axis, [(source, source + steps) for source in range(l...  64.3 us
    all_gather x1, blocking collectives, on_device(): lax.all_gather(out_grad, 'head', axis=1, tiled=True)  23.3 us
    dot_general x6, matrix products, head_step(): jnp.einsum('qk,qd->kd', score_grad, query_head, preferred_element_type=jn...  12.8 us
  transfers between devices with their start and end apart: 17, of which 7 were waited for; matrix products, arithmetic and copies ran while one was open for 3% of the time, Pallas kernels for 0%

commit v1 on v0

v1 whole, which is shorter than its diff:
```python
import jax
import jax.numpy as jnp
from jax import lax
from jax.experimental import pallas as pl
from jax.experimental.pallas import tpu as pltpu
from jax.sharding import PartitionSpec as P

HD = 128
GT = 4
GH = 16
T = 160
NH = 3
HALF = NH * HD
FULL = 2 * HALF
WIN = 9 * T
SIDE = 3 * T
MESH = pl.DeviceIdType.MESH
BF = jnp.bfloat16
F32 = jnp.float32


def nt(a, b):
    return lax.dot_general(a, b, (((1,), (1,)), ((), ())), preferred_element_type=F32)


def nn(a, b):
    return lax.dot_general(a, b, (((1,), (0,)), ((), ())), preferred_element_type=F32)


def tn(a, b):
    return lax.dot_general(a, b, (((0,), (0,)), ((), ())), preferred_element_type=F32)


def kernel(
    q_in, k_in, v_in, w_in, g_in, valid,
    mixed, dq_out, dk_out, dv_out,
    kv, kvo, qo, qb, dob, dop, gall, wm, wo, att, attr, dqb, pb, bias,
    xs, rx, acc, zs, rz, ys, ms, mr, ms2, mr2, mo, rb, rb2, rc,
    lsem, hsem, fs, fr, bxs, bxr, bzs, bzr, bys, byr, gs, gr, qs, qr, dqs, dqr, ats, atr, mss, msr, rls, rlr, bcs, bcr,
):
    i = lax.axis_index("tile")
    j = lax.axis_index("head")
    t = i // GH
    g = i % GH
    p = g % 2
    u = g // 2
    d = 2 * p - 1
    e = (u == 3).astype(jnp.int32) - (u == 4).astype(jnp.int32)
    near = (t * GH + (g + 2 * d + GH) % GH, j)
    far = (t * GH + (g - 2 * d + GH) % GH, j)
    up = (((t + 1) % GT) * GH + g, j)
    down = (((t + GT - 1) % GT) * GH + g, j)
    relay = (t * GH + (g + GH // 2) % GH, j)
    relay_to = (t * GH + (g + 6 + 4 * (u == 7).astype(jnp.int32)) % GH, j)
    back = (((t - e + GT) % GT) * GH + (g + 2 * e), j)
    j1 = j + 1 - 2 * (j % 2)
    j2 = (j + 2) % 4
    partner = (i + 1 - 2 * p, j2)
    j3 = (j1 + 2) % 4
    sibling = (i, j1)
    across = (i, j2)
    has_up = t < GT - 1
    has_down = t > 0
    has_near = (u + d >= 0) & (u + d < GH // 2)
    has_far = (u - d >= 0) & (u - d < GH // 2)
    near_cross = e == d
    far_cross = e == -d
    is_cross = e != 0
    is_relay = (u == 0) | (u == 7)
    has_back = (t - e >= 0) & (t - e < GT)
    has_ahead = (t + e >= 0) & (t + e < GT)
    mine = pl.multiple_of(p * HALF, 128)
    theirs = pl.multiple_of((1 - p) * HALF, 128)
    scale = HD ** (-0.5)

    @pl.when(jnp.logical_not(has_down))
    def _():
        for s in (0, 3, 6, 9):
            kv[:, pl.ds(s * T, T), :] = jnp.zeros((NH, T, 2 * HD), BF)
        rz[:, 1] = jnp.zeros((NH, 2 * T, 2 * HD), BF)

    @pl.when(jnp.logical_not(has_up))
    def _():
        for s in (2, 5, 8, 11):
            kv[:, pl.ds(s * T, T), :] = jnp.zeros((NH, T, 2 * HD), BF)
        rz[:, 0] = jnp.zeros((NH, 2 * T, 2 * HD), BF)

    for n, side, there, crossing in ((0, 0, has_near, near_cross), (1, 3, has_far, far_cross)):
        @pl.when(jnp.logical_not(there))
        def _():
            kv[:, pl.ds(side * SIDE, SIDE), :] = jnp.zeros((NH, SIDE, 2 * HD), BF)

        @pl.when(jnp.logical_not(there) | crossing)
        def _():
            rx[:, n] = jnp.zeros((NH, SIDE, 2 * HD), BF)

    barrier = pltpu.get_barrier_semaphore()
    greeted = 0
    for peer, cond in (
        (partner, None), (sibling, None), (across, None), (near, has_near), (far, has_far), (up, has_up),
        (down, has_down), (relay, is_cross | is_relay), (relay_to, is_relay),
        ((t * GH + (g + GH - 6 * e) % GH, j), is_cross), (back, is_cross & has_back),
    ):
        if cond is None:
            pl.semaphore_signal(barrier, inc=1, device_id=peer, device_id_type=MESH)
            greeted += 1
        else:
            @pl.when(cond)
            def _():
                pl.semaphore_signal(barrier, inc=1, device_id=peer, device_id_type=MESH)
            greeted += cond.astype(jnp.int32)

    START, WAIT = 0, 1

    def when(cond, action):
        if cond is None:
            action()
        else:
            @pl.when(cond)
            def _():
                action()

    def remote(act, src, dst, send, recv, device, cond=None):
        copy = pltpu.make_async_remote_copy(
            src_ref=src, dst_ref=dst, send_sem=send, recv_sem=recv, device_id=device, device_id_type=MESH
        )
        when(cond, copy.start if act == START else copy.wait_send)

    def arrived(dst, recv, cond=None):
        copy = pltpu.make_async_remote_copy(
            src_ref=dst, dst_ref=dst, send_sem=lsem.at[0], recv_sem=recv, device_id=partner, device_id_type=MESH
        )
        when(cond, copy.wait_recv)

    def slot(h, s):
        return kv.at[h, pl.ds(s * T, T), :]

    def cols(h):
        return pl.ds(pl.multiple_of(h * HD, HD), HD)

    def mine_cols(h):
        return pl.ds(pl.multiple_of(mine + h * HD, HD), HD)

    def their_cols(h):
        return pl.ds(pl.multiple_of(theirs + h * HD, HD), HD)

    def local(src, dst, sem):
        copy = pltpu.make_async_copy(src, dst, sem)
        copy.start()
        return copy

    staged = [
        [
            local(source.at[:, columns(h)], kvo.at[h, n, :, pl.ds(part * HD, HD)], hsem.at[h, 2 * n + part])
            for n, columns in enumerate((mine_cols, their_cols))
            for part, source in enumerate((k_in, v_in))
        ]
        for h in range(NH)
    ]
    g_copy = local(g_in, gall.at[0], lsem.at[0])
    q_copies = [
        local(q_in.at[:, pl.ds(mine, HALF)], qo.at[0], lsem.at[1]),
        local(q_in.at[:, pl.ds(theirs, HALF)], qo.at[1], lsem.at[2]),
    ]
    w_copies = [
        local(w_in.at[:, pl.ds(theirs, HALF)], wo, lsem.at[3]),
        local(w_in.at[:, pl.ds(mine, HALF)], wm, lsem.at[4]),
    ]

    lanes = lax.broadcasted_iota(jnp.int32, (1, WIN), 1)
    for a in range(2):
        row = jnp.zeros((1, WIN), F32)
        for n in range(9):
            g_slot, t_slot = a + n // 3, n % 3
            t_abs = t + t_slot - 1
            g_abs = g + (g_slot - 1) * (1 - 2 * p)
            if t_slot == 1 and g_slot == a + 1:
                value = jnp.float32(0.0)
            else:
                flag = valid[((t_abs + GT) % GT) * GH + (g_abs + GH) % GH]
                inside = (t_abs >= 0) & (t_abs < GT) & (g_abs >= 0) & (g_abs < GH)
                value = jnp.where(inside & (flag > 0), 0.0, -jnp.inf).astype(F32)
            row = jnp.where((lanes >= n * T) & (lanes < (n + 1) * T), value, row)
        bias[a] = row

    pl.semaphore_wait(barrier, greeted)

    def send_side(act, h, s, target, n, device, there, crossing):
        tile = slot(h, s)
        remote(act, tile, slot(h, target), fs.at[h, n], fr.at[h, target], device, there & jnp.logical_not(crossing))
        remote(act, tile, rb.at[h], rls.at[h, 0], rlr.at[h, 0], relay, crossing)
        remote(
            act, tile, slot(h, target + e), fs.at[h, n + 1], fr.at[h, target + e], back, crossing & has_back
        )

    def send_swap(act, h):
        remote(act, kvo.at[h, 0], slot(h, 4), fs.at[h, 12], fr.at[h, 4], across)
        remote(act, kvo.at[h, 1], slot(h, 7), fs.at[h, 13], fr.at[h, 7], partner)

    def send_z(act, h, s):
        remote(act, slot(h, s), slot(h, s - 1), fs.at[h, 0 if s == 4 else 2], fr.at[h, s - 1], up, has_up)
        remote(act, slot(h, s), slot(h, s + 1), fs.at[h, 1 if s == 4 else 3], fr.at[h, s + 1], down, has_down)

    def send_own_x(act, h):
        send_side(act, h, 4, 10, 4, near, has_near, near_cross)

    def send_other_x(act, h):
        send_side(act, h, 7, 1, 6, far, has_far, far_cross)

    def pass_on(act, h):
        target = jnp.where((u == 7) == (p == 1), 10, 1)
        remote(act, rb.at[h], slot(h, target), rls.at[h, 1], fr.at[h, target], relay_to, is_relay)

    def forward(act, h, n):
        target, device, there, crossing = ((9, near, has_near, near_cross), (0, far, has_far, far_cross))[n]
        for k, exists, way in ((0, has_down, 1), (2, has_up, -1)):
            source = slot(h, 3 + 3 * n + k)
            if act == START:
                arrived(source, fr.at[h, 3 + 3 * n + k], exists)
            remote(
                act, source, slot(h, target + k), fs.at[h, 8 + 2 * n + k // 2], fr.at[h, target + k], device,
                exists & there & (jnp.logical_not(crossing) | (e == way)),
            )

    def send_back(act, h, n):
        device, there, crossing = ((far, has_far, far_cross), (near, has_near, near_cross))[n]
        remote(
            act, xs.at[h, n], rx.at[h, n], bxs.at[h, n, 0], bxr.at[h, n, 0], device,
            there & jnp.logical_not(crossing),
        )
        remote(act, xs.at[h, n, pl.ds(T, T)], rb2.at[h], rls.at[h, 2], rlr.at[h, 1], relay, crossing)
        rows = pl.ds((1 + e) * T, T)
        remote(
            act, xs.at[h, n, rows], rx.at[h, n, rows], bxs.at[h, n, 1], bxr.at[h, n, 2], device, crossing & has_ahead
        )
        remote(
            act, xs.at[h, n, pl.ds((1 - e) * T, T)], rc.at[h], bcs.at[h, n], bcr.at[h], back, crossing & has_back
        )

    def pass_back(act, h):
        n = jnp.where(u == 7, p, 1 - p)
        remote(act, rb2.at[h], rx.at[h, n, pl.ds(T, T)], rls.at[h, 3], bxr.at[h, n, 1], relay_to, is_relay)

    def send_attended(act, h):
        for n, device in enumerate((across, partner)):
            remote(act, att.at[n, :, cols(h)], attr.at[n, :, cols(h)], ats.at[h, n], atr.at[h, n], device)

    def send_query_grad(act, h):
        for n, device in enumerate((across, partner)):
            remote(act, dqb.at[n, :, cols(h)], dq_out.at[:, mine_cols(h)], dqs.at[h, n], dqr.at[h, n], device)

    def send_reduced(act, h):
        remote(act, zs.at[h, 0], rz.at[h, 0], bzs.at[h, 0], bzr.at[h, 0], down, has_down)
        remote(act, zs.at[h, 1], rz.at[h, 1], bzs.at[h, 1], bzr.at[h, 1], up, has_up)

    def send_total(act, h):
        for n, device in enumerate((across, partner)):
            for part, out in enumerate((dk_out, dv_out)):
                remote(
                    act, ys.at[h, n, :, pl.ds(part * HD, HD)], out.at[:, mine_cols(h)], bys.at[h, n, part],
                    byr.at[h, n, part], device,
                )

    def attend(h):
        for s, there in ((9, has_far & has_down), (10, has_far), (11, has_far & has_up),
                         (0, has_near & has_down), (1, has_near), (2, has_near & has_up)):
            arrived(slot(h, s), fr.at[h, s], there)
        for a in range(2):
            window = pl.ds(a * SIDE, WIN)
            s = nt(qb[a, :, cols(h)], kv[h, window, pl.ds(0, HD)]) * scale + bias[a]
            x = jnp.exp(s - jnp.max(s, axis=1, keepdims=True))
            weights = (x * (1.0 / jnp.sum(x, axis=1, keepdims=True))).astype(BF)
            pb[a] = weights
            att[a, :, cols(h)] = nn(weights, kv[h, window, pl.ds(HD, HD)]).astype(BF)
        send_attended(START, h)

    def differentiate(h, a):
        q = qb[a, :, cols(h)]
        do = dob[a, :, cols(h)]
        window = pl.ds(a * SIDE, WIN)
        k = kv[h, window, pl.ds(0, HD)]
        weights = pb[a]
        row_dot = jnp.sum(do.astype(F32) * att[a, :, cols(h)].astype(F32), axis=1, keepdims=True)
        weight_grad = nt(do, kv[h, window, pl.ds(HD, HD)])
        score_grad = (weights.astype(F32) * (weight_grad - row_dot) * scale).astype(BF)
        dqb[a, :, cols(h)] = nn(score_grad, k).astype(BF)
        for part, lhs, rhs in ((0, score_grad, q), (1, weights, do)):
            grad = tn(lhs, rhs)
            lane = pl.ds(part * HD, HD)
            if a == 0:
                xs[h, 1, :, lane] = grad[:SIDE].astype(BF)
                acc[h, :, lane] = grad[SIDE:]
            else:
                acc[h, :, lane] += grad[:2 * SIDE]
                xs[h, 0, :, lane] = grad[2 * SIDE:].astype(BF)
        send_back(START, h, 1 - a)
        if a == 1:
            send_query_grad(START, h)

    def reduce_x(h):
        for n, there, crossing in ((0, has_near, near_cross), (1, has_far, far_cross)):
            arrived(rx.at[h, n], bxr.at[h, n, 0], there & jnp.logical_not(crossing))
            arrived(rx.at[h, n, pl.ds(T, T)], bxr.at[h, n, 1], crossing)
            arrived(rx.at[h, n, pl.ds((1 - e) * T, T)], bxr.at[h, n, 2], crossing & has_back)
        for n in range(2):
            for part, row in ((0, 0), (1, 2 * T)):
                zs[h, part, pl.ds(n * T, T), :] = (
                    acc[h, pl.ds(n * SIDE + row, T), :] + rx[h, n, pl.ds(row, T), :].astype(F32)
                ).astype(BF)
            acc[h, pl.ds(n * SIDE + T, T), :] += rx[h, n, pl.ds(T, T), :].astype(F32)
        send_reduced(START, h)

    def reduce_z(h):
        arrived(rz.at[h, 0], bzr.at[h, 0], has_up)
        arrived(rz.at[h, 1], bzr.at[h, 1], has_down)
        arrived(rc.at[h], bcr.at[h], is_cross & has_back)
        for n, crossing in ((0, near_cross), (1, far_cross)):
            @pl.when(crossing & has_back)
            def _():
                acc[h, pl.ds(n * SIDE + T, T), :] += rc[h].astype(F32)

        for n in range(2):
            rows = pl.ds(n * T, T)
            ys[h, n] = (
                acc[h, pl.ds(n * SIDE + T, T), :] + rz[h, 0, rows, :].astype(F32) + rz[h, 1, rows, :].astype(F32)
            ).astype(BF)
        send_total(START, h)

    blocks = (j, j1, j2, j3)
    rows = [pl.ds(pl.multiple_of(block * FULL, FULL), FULL) for block in blocks]

    def attn_grad(weights_ref):
        total = nn(gall[0], weights_ref[rows[0], :])
        for n in range(1, 4):
            total = total + nn(gall[n], weights_ref[rows[n], :])
        return total.astype(BF)

    blocks = (j, j1, j2, j3)
    rows = [pl.ds(pl.multiple_of(block * FULL, FULL), FULL) for block in blocks]

    def send_gathered(act, n):
        source, target, device, k = ((0, 2, across, 1), (0, 1, sibling, 0), (2, 3, sibling, 2))[n]
        remote(act, gall.at[source], gall.at[target], gs.at[k], gr.at[k], device)

    def send_queries(act):
        for n, device in enumerate((across, partner)):
            remote(act, qo.at[n], qb.at[n], qs.at[n], qr.at[n], device)

    def send_attn_grad(n):
        weights_ref = (wm, wo)[n]
        total = nn(gall[0], weights_ref[rows[0], :])
        for k in range(1, 4):
            total = total + nn(gall[k], weights_ref[rows[k], :])
        dop[n] = total.astype(BF)
        remote(START, dop.at[n], dob.at[n], qs.at[2 + n], qr.at[2 + n], (across, partner)[n])

    def project(n):
        return nt(attr[0], wm[rows[n], :]) + nt(attr[1], wo[rows[n], :])

    for copy in staged[0]:
        copy.wait()
    send_swap(START, 0)
    g_copy.wait()
    send_gathered(START, 1)
    arrived(slot(0, 7), fr.at[0, 7])
    send_z(START, 0, 7)
    arrived(slot(0, 4), fr.at[0, 4])
    send_z(START, 0, 4)
    for copy in staged[1]:
        copy.wait()
    send_swap(START, 1)
    send_own_x(START, 0)
    send_gathered(START, 0)
    send_other_x(START, 0)
    arrived(gall.at[2], gr.at[1])
    send_gathered(START, 2)
    arrived(slot(1, 7), fr.at[1, 7])
    send_z(START, 1, 7)
    for copy in q_copies:
        copy.wait()
    send_queries(START)
    for copy in staged[2]:
        copy.wait()
    send_swap(START, 2)
    forward(START, 0, 1)
    arrived(rb.at[0], rlr.at[0, 0], is_relay)
    pass_on(START, 0)
    forward(START, 0, 0)
    send_other_x(START, 1)
    send_z(WAIT, 0, 4)
    for copy in w_copies:
        copy.wait()
    arrived(gall.at[1], gr.at[0])
    arrived(gall.at[3], gr.at[2])
    send_attn_grad(1)
    send_attn_grad(0)
    arrived(slot(1, 4), fr.at[1, 4])
    send_z(START, 1, 4)
    send_z(WAIT, 0, 7)
    send_own_x(START, 1)
    for n in range(2):
        arrived(qb.at[n], qr.at[n])
    attend(0)
    for n in range(2):
        arrived(dob.at[n], qr.at[2 + n])
    differentiate(0, 0)
    differentiate(0, 1)
    forward(START, 1, 0)
    forward(START, 1, 1)
    arrived(slot(2, 4), fr.at[2, 4])
    send_z(START, 2, 4)
    arrived(rb2.at[0], rlr.at[0, 1], is_relay)
    pass_back(START, 0)
    arrived(slot(2, 7), fr.at[2, 7])
    send_z(START, 2, 7)
    arrived(rb.at[1], rlr.at[1, 0], is_relay)
    pass_on(START, 1)
    send_own_x(START, 2)
    attend(1)
    send_other_x(START, 2)
    send_z(WAIT, 1, 7)
    forward(START, 2, 0)
    reduce_x(0)
    forward(START, 2, 1)
    send_z(WAIT, 2, 7)
    differentiate(1, 0)
    send_z(WAIT, 2, 4)
    send_z(WAIT, 1, 4)
    differentiate(1, 1)
    arrived(rb.at[2], rlr.at[2, 0], is_relay)
    pass_on(START, 2)
    attend(2)
    differentiate(2, 0)
    arrived(rb2.at[1], rlr.at[1, 1], is_relay)
    pass_back(START, 1)
    reduce_x(1)
    differentiate(2, 1)
    arrived(rb2.at[2], rlr.at[2, 1], is_relay)
    pass_back(START, 2)
    reduce_z(0)
    reduce_x(2)
    for h in range(NH):
        for n in range(2):
            arrived(attr.at[n, :, cols(h)], atr.at[h, n])
    ms[0] = project(3).astype(BF)
    ms[1] = project(1).astype(BF)
    remote(START, ms, mr, mss.at[0], msr.at[0], sibling)
    reduce_z(1)
    crossing_sum = project(2)
    arrived(mr, msr.at[0])
    ms2[...] = (crossing_sum + mr[0].astype(F32)).astype(BF)
    remote(START, ms2, mr2, mss.at[1], msr.at[1], across)
    kept = project(0) + mr[1].astype(F32)
    reduce_z(2)
    arrived(mr2, msr.at[1])
    mo[...] = (kept + mr2[...].astype(F32)).astype(BF)
    mixed_copy = local(mo, mixed, lsem.at[5])

    for n in range(3):
        send_gathered(WAIT, n)
    send_queries(WAIT)
    for n, device in enumerate((across, partner)):
        remote(WAIT, dop.at[n], dob.at[n], qs.at[2 + n], qr.at[2 + n], device)
    remote(WAIT, ms, mr, mss.at[0], msr.at[0], sibling)
    remote(WAIT, ms2, mr2, mss.at[1], msr.at[1], across)
    for h in range(NH):
        for send in (
            send_swap, send_own_x, send_other_x, pass_on, pass_back, send_attended, send_query_grad, send_reduced,
            send_total,
        ):
            send(WAIT, h)
        for n, columns in enumerate((mine_cols, their_cols)):
            forward(WAIT, h, n)
            send_back(WAIT, h, n)
            arrived(dq_out.at[:, columns(h)], dqr.at[h, n])
            arrived(dk_out.at[:, columns(h)], byr.at[h, n, 0])
            arrived(dv_out.at[:, columns(h)], byr.at[h, n, 1])
    mixed_copy.wait()

def hand_over(*refs):
    for n in range(4):
        refs[4 + n][...] = refs[n][...]


def on_device(queries, keys, values, w_out, out_grad, tile_valid):
    dma = pltpu.SemaphoreType.DMA
    any_space = pl.BlockSpec(memory_space=pl.ANY)
    block = jax.ShapeDtypeStruct(queries.shape, BF)
    results = pl.pallas_call(
        kernel,
        out_shape=(block, block, block, block),
        in_specs=[any_space] * 5 + [pl.BlockSpec(memory_space=pltpu.SMEM)],
        out_specs=(any_space, any_space, any_space, any_space),
        scratch_shapes=[
            pltpu.VMEM((NH, 12 * T, 2 * HD), BF),
            pltpu.VMEM((NH, 2, T, 2 * HD), BF),
            pltpu.VMEM((2, T, HALF), BF),
            pltpu.VMEM((2, T, HALF), BF),
            pltpu.VMEM((2, T, HALF), BF),
            pltpu.VMEM((2, T, HALF), BF),
            pltpu.VMEM((4, T, FULL), BF),
            pltpu.VMEM((4 * FULL, HALF), BF),
            pltpu.VMEM((4 * FULL, HALF), BF),
            pltpu.VMEM((2, T, HALF), BF),
            pltpu.VMEM((2, T, HALF), BF),
            pltpu.VMEM((2, T, HALF), BF),
            pltpu.VMEM((2, T, WIN), BF),
            pltpu.VMEM((2, 1, WIN), F32),
            pltpu.VMEM((NH, 2, SIDE, 2 * HD), BF),
            pltpu.VMEM((NH, 2, SIDE, 2 * HD), BF),
            pltpu.VMEM((NH, 2 * SIDE, 2 * HD), F32),
            pltpu.VMEM((NH, 2, 2 * T, 2 * HD), BF),
            pltpu.VMEM((NH, 2, 2 * T, 2 * HD), BF),
            pltpu.VMEM((NH, 2, T, 2 * HD), BF),
            pltpu.VMEM((2, T, FULL), BF),
            pltpu.VMEM((2, T, FULL), BF),
            pltpu.VMEM((T, FULL), BF),
            pltpu.VMEM((T, FULL), BF),
            pltpu.VMEM((T, FULL), BF),
            pltpu.VMEM((NH, T, 2 * HD), BF),
            pltpu.VMEM((NH, T, 2 * HD), BF),
            pltpu.VMEM((NH, T, 2 * HD), BF),
            dma((6,)),
            dma((NH, 4)),
            dma((NH, 14)),
            dma((NH, 12)),
            dma((NH, 2, 2)),
            dma((NH, 2, 3)),
            dma((NH, 2)),
            dma((NH, 2)),
            dma((NH, 2, 2)),
            dma((NH, 2, 2)),
            dma((3,)),
            dma((3,)),
            dma((4,)),
            dma((4,)),
            dma((NH, 2)),
            dma((NH, 2)),
            dma((NH, 2)),
            dma((NH, 2)),
            dma((2,)),
            dma((2,)),
            dma((NH, 4)),
            dma((NH, 2)),
            dma((NH, 2)),
            dma((NH,)),
        ],
        compiler_params=pltpu.CompilerParams(
            collective_id=0, has_side_effects=True, vmem_limit_bytes=56 * 1024 * 1024
        ),
    )(queries, keys, values, w_out, out_grad, tile_valid)
    whole = pl.BlockSpec(memory_space=pltpu.VMEM)
    return pl.pallas_call(
        hand_over,
        out_shape=(block, block, block, block),
        in_specs=[whole] * 4,
        out_specs=(whole, whole, whole, whole),
    )(*results)


def solution(mesh):
    return jax.shard_map(
        on_device,
        mesh=mesh,
        in_specs=(
            P("tile", "head"),
            P("tile", "head"),
            P("tile", "head"),
            P(None, "head"),
            P("tile", "head"),
            P(),
        ),
        out_specs=(P("tile", "head"), P("tile", "head"), P("tile", "head"), P("tile", "head")),
        check_vma=False,
    )
```

time: 435 us -> 97.5 us (0.22)
  the two profiles are of different devices: /device:TPU:183 before, /device:TPU:161 now
where the time goes in v1:
time: 97.5 us; the launch traced here: 97.4 us
  Pallas kernels  96.8 us (99%)
    pallas_call x1, Pallas kernels, on_device(): pl.pallas_call(kernel, out_shape=(block, block, block, block), in_specs=[...  94.5 us
    pallas_call x1, Pallas kernels, on_device(): pl.pallas_call(hand_over, out_shape=(block, block, block, block), in_spec...  2.27 us

profile of v1, /device:TPU:161, one launch (start us, length us, event | category | flops | bytes accessed | tf_op | source)
XLA Modules:
  0.0 97.4 jit_solution(11897290429392465422)
XLA Ops:
  0.6 94.5 %shard_map.93 = (bf16[160,768]{1,0:T(8,128)(2,1)}, bf16[160,768]{1,0:T(8,128)(2,1)}, bf16[160,768]{1,0:T(8,128)(2,1)}, bf16[160,768]{1,0:T(8,128)(2,1)}) custom-call(bf16[160,768]{1,0:T(8,128)(2,1)} %q_in.1, bf16[160,768]{1,0:T(8,128)(2,1)} %k_in.1, bf16[160,768]{1,0:T(8,128)(2,1)} %v_in.1, bf16[3072,768]{1,0:T(8,128)(2,1)} %w_in.1, bf16[160,768]{1,0:T(8,128)(2,1)} %g_in.1, ...), custom_call_target="tpu_custom_call" | custom-call | tf_op jit(solution)/shard_map/pallas_call | solution.py:489
  95.1 2.3 %shard_map.94 = (bf16[160,768]{1,0:T(8,128)(2,1)}, bf16[160,768]{1,0:T(8,128)(2,1)}, bf16[160,768]{1,0:T(8,128)(2,1)}, bf16[160,768]{1,0:T(8,128)(2,1)}) custom-call(bf16[160,768]{1,0:T(8,128)(2,1)} %get-tuple-element.8.refs_0_, bf16[160,768]{1,0:T(8,128)(2,1)} %get-tuple-element.9.refs_1_, bf16[160,768]{1,0:T(8,128)(2,1)} %get-tuple-element.10.refs_2_, ...), custom_call_target="tpu_custom_call" | custom-call | tf_op jit(solution)/shard_map/pallas_call | solution.py:553

commit v2 on v1

--- a/solution.py
+++ b/solution.py
@@ -357,47 +357,57 @@
     def project(n):
         return nt(attr[0], wm[rows[n], :]) + nt(attr[1], wo[rows[n], :])
 
+    g_copy.wait()
+    send_gathered(START, 0)
+    send_gathered(START, 1)
     for copy in staged[0]:
         copy.wait()
     send_swap(START, 0)
-    g_copy.wait()
-    send_gathered(START, 1)
-    arrived(slot(0, 7), fr.at[0, 7])
-    send_z(START, 0, 7)
-    arrived(slot(0, 4), fr.at[0, 4])
-    send_z(START, 0, 4)
     for copy in staged[1]:
         copy.wait()
     send_swap(START, 1)
+    for copy in staged[2]:
+        copy.wait()
+    send_swap(START, 2)
+    arrived(slot(0, 4), fr.at[0, 4])
+    send_z(START, 0, 4)
     send_own_x(START, 0)
-    send_gathered(START, 0)
+    arrived(slot(0, 7), fr.at[0, 7])
+    send_z(START, 0, 7)
     send_other_x(START, 0)
+    arrived(slot(1, 4), fr.at[1, 4])
+    send_z(START, 1, 4)
+    send_own_x(START, 1)
+    for copy in q_copies:
+        copy.wait()
+    send_queries(START)
     arrived(gall.at[2], gr.at[1])
     send_gathered(START, 2)
     arrived(slot(1, 7), fr.at[1, 7])
     send_z(START, 1, 7)
-    for copy in q_copies:
-        copy.wait()
-    send_queries(START)
-    for copy in staged[2]:
-        copy.wait()
-    send_swap(START, 2)
-    forward(START, 0, 1)
+    send_other_x(START, 1)
+    arrived(slot(2, 4), fr.at[2, 4])
+    send_z(START, 2, 4)
+    send_own_x(START, 2)
     arrived(rb.at[0], rlr.at[0, 0], is_relay)
     pass_on(START, 0)
-    forward(START, 0, 0)
-    send_other_x(START, 1)
-    send_z(WAIT, 0, 4)
     for copy in w_copies:
         copy.wait()
     arrived(gall.at[1], gr.at[0])
     arrived(gall.at[3], gr.at[2])
     send_attn_grad(1)
     send_attn_grad(0)
-    arrived(slot(1, 4), fr.at[1, 4])
-    send_z(START, 1, 4)
-    send_z(WAIT, 0, 7)
-    send_own_x(START, 1)
+    arrived(slot(2, 7), fr.at[2, 7])
+    send_z(START, 2, 7)
+    send_other_x(START, 2)
+    arrived(rb.at[1], rlr.at[1, 0], is_relay)
+    pass_on(START, 1)
+    forward(START, 0, 0)
+    forward(START, 0, 1)
+    arrived(rb.at[2], rlr.at[2, 0], is_relay)
+    pass_on(START, 2)
+    forward(START, 1, 0)
+    forward(START, 1, 1)
     for n in range(2):
         arrived(qb.at[n], qr.at[n])
     attend(0)
@@ -405,56 +415,46 @@
         arrived(dob.at[n], qr.at[2 + n])
     differentiate(0, 0)
     differentiate(0, 1)
-    forward(START, 1, 0)
-    forward(START, 1, 1)
-    arrived(slot(2, 4), fr.at[2, 4])
-    send_z(START, 2, 4)
+    forward(START, 2, 0)
+    forward(START, 2, 1)
+    attend(1)
+    differentiate(1, 0)
+    differentiate(1, 1)
     arrived(rb2.at[0], rlr.at[0, 1], is_relay)
     pass_back(START, 0)
-    arrived(slot(2, 7), fr.at[2, 7])
-    send_z(START, 2, 7)
-    arrived(rb.at[1], rlr.at[1, 0], is_relay)
-    pass_on(START, 1)
-    send_own_x(START, 2)
-    attend(1)
-    send_other_x(START, 2)
-    send_z(WAIT, 1, 7)
-    forward(START, 2, 0)
     reduce_x(0)
-    forward(START, 2, 1)
-    send_z(WAIT, 2, 7)
-    differentiate(1, 0)
-    send_z(WAIT, 2, 4)
-    send_z(WAIT, 1, 4)
-    differentiate(1, 1)
-    arrived(rb.at[2], rlr.at[2, 0], is_relay)
-    pass_on(START, 2)
     attend(2)
     differentiate(2, 0)
+    differentiate(2, 1)
     arrived(rb2.at[1], rlr.at[1, 1], is_relay)
     pass_back(START, 1)
     reduce_x(1)
-    differentiate(2, 1)
-    arrived(rb2.at[2], rlr.at[2, 1], is_relay)
-    pass_back(START, 2)
     reduce_z(0)
-    reduce_x(2)
     for h in range(NH):
         for n in range(2):
             arrived(attr.at[n, :, cols(h)], atr.at[h, n])
     ms[0] = project(3).astype(BF)
     ms[1] = project(1).astype(BF)
     remote(START, ms, mr, mss.at[0], msr.at[0], sibling)
-    reduce_z(1)
+    arrived(rb2.at[2], rlr.at[2, 1], is_relay)
+    pass_back(START, 2)
+    reduce_x(2)
     crossing_sum = project(2)
     arrived(mr, msr.at[0])
     ms2[...] = (crossing_sum + mr[0].astype(F32)).astype(BF)
     remote(START, ms2, mr2, mss.at[1], msr.at[1], across)
     kept = project(0) + mr[1].astype(F32)
-    reduce_z(2)
+    reduce_z(1)
     arrived(mr2, msr.at[1])
     mo[...] = (kept + mr2[...].astype(F32)).astype(BF)
     mixed_copy = local(mo, mixed, lsem.at[5])
+    reduce_z(2)
+    send_z(WAIT, 0, 4)
+    send_z(WAIT, 0, 7)
+    send_z(WAIT, 1, 4)
+    send_z(WAIT, 1, 7)
+    send_z(WAIT, 2, 4)
+    send_z(WAIT, 2, 7)
 
     for n in range(3):
         send_gathered(WAIT, n)

time: 97.5 us -> 94.6 us (0.970)
  the two profiles are of different devices: /device:TPU:161 before, /device:TPU:32 now
where the time goes in v2:
time: 94.6 us; the launch traced here: 94.4 us
  Pallas kernels  93.8 us (99%)
    pallas_call x1, Pallas kernels, on_device(): pl.pallas_call(kernel, out_shape=(block, block, block, block), in_specs=[...  91.5 us
    pallas_call x1, Pallas kernels, on_device(): pl.pallas_call(hand_over, out_shape=(block, block, block, block), in_spec...  2.27 us

profile of v2, /device:TPU:32, one launch (start us, length us, event | category | flops | bytes accessed | tf_op | source)
XLA Modules:
  0.0 94.4 jit_solution(13998477984177096810)
XLA Ops:
  0.6 91.5 %shard_map.93 = (bf16[160,768]{1,0:T(8,128)(2,1)}, bf16[160,768]{1,0:T(8,128)(2,1)}, bf16[160,768]{1,0:T(8,128)(2,1)}, bf16[160,768]{1,0:T(8,128)(2,1)}) custom-call(bf16[160,768]{1,0:T(8,128)(2,1)} %q_in.1, bf16[160,768]{1,0:T(8,128)(2,1)} %k_in.1, bf16[160,768]{1,0:T(8,128)(2,1)} %v_in.1, bf16[3072,768]{1,0:T(8,128)(2,1)} %w_in.1, bf16[160,768]{1,0:T(8,128)(2,1)} %g_in.1, ...), custom_call_target="tpu_custom_call" | custom-call | tf_op jit(solution)/shard_map/pallas_call | solution.py:489
  92.2 2.3 %shard_map.94 = (bf16[160,768]{1,0:T(8,128)(2,1)}, bf16[160,768]{1,0:T(8,128)(2,1)}, bf16[160,768]{1,0:T(8,128)(2,1)}, bf16[160,768]{1,0:T(8,128)(2,1)}) custom-call(bf16[160,768]{1,0:T(8,128)(2,1)} %get-tuple-element.8.refs_0_, bf16[160,768]{1,0:T(8,128)(2,1)} %get-tuple-element.9.refs_1_, bf16[160,768]{1,0:T(8,128)(2,1)} %get-tuple-element.10.refs_2_, ...), custom_call_target="tpu_custom_call" | custom-call | tf_op jit(solution)/shard_map/pallas_call | solution.py:553

commit v3 on v2

v3 whole, which is shorter than its diff:
```python
import jax
import jax.numpy as jnp
from jax import lax
from jax.experimental import pallas as pl
from jax.experimental.pallas import tpu as pltpu
from jax.sharding import PartitionSpec as P

HD = 128
GT = 4
GH = 16
T = 160
NH = 3
HALF = NH * HD
FULL = 2 * HALF
WIN = 9 * T
SIDE = 3 * T
MESH = pl.DeviceIdType.MESH
BF = jnp.bfloat16
F32 = jnp.float32


def nt(a, b):
    return lax.dot_general(a, b, (((1,), (1,)), ((), ())), preferred_element_type=F32)


def nn(a, b):
    return lax.dot_general(a, b, (((1,), (0,)), ((), ())), preferred_element_type=F32)


def tn(a, b):
    return lax.dot_general(a, b, (((0,), (0,)), ((), ())), preferred_element_type=F32)


def kernel(
    q_in, k_in, v_in, w_in, g_in, valid,
    mixed, dq_out, dk_out, dv_out,
    kv, kvo, qb, dob, dop, gall, wm, wo, att, attr, dqb, bias,
    xs, rx, acc, zs, rz, yo, ys, ms, mr, ms2, mr2, mo, rb, rb2, rc, pb, qo,
    lsem, fs, fr, bxs, bxr, bzs, bzr, bys, byr, gs, gr, qs, qr, ats, atr, mss, msr, rls, rlr, bcs, bcr,
):
    i = lax.axis_index("tile")
    j = lax.axis_index("head")
    t = i // GH
    g = i % GH
    p = g % 2
    u = g // 2
    d = 2 * p - 1
    e = (u == 3).astype(jnp.int32) - (u == 4).astype(jnp.int32)
    partner = (i + 1 - 2 * p, j)
    near = (t * GH + (g + 2 * d + GH) % GH, j)
    far = (t * GH + (g - 2 * d + GH) % GH, j)
    up = (((t + 1) % GT) * GH + g, j)
    down = (((t + GT - 1) % GT) * GH + g, j)
    eight_off = (t * GH + (g + GH // 2) % GH, j)
    six_off = (t * GH + (g + 6 + 4 * (u == 7).astype(jnp.int32)) % GH, j)
    relay = (t * GH + (g + GH - 6 * e) % GH, j)
    relay_to = eight_off
    back = (((t - e + GT) % GT) * GH + (g + 2 * e), j)
    j1 = j + 1 - 2 * (j % 2)
    j2 = (j + 2) % 4
    j3 = (j1 + 2) % 4
    sibling = (i, j1)
    across = (i, j2)
    has_up = t < GT - 1
    has_down = t > 0
    has_near = (u + d >= 0) & (u + d < GH // 2)
    has_far = (u - d >= 0) & (u - d < GH // 2)
    near_cross = e == d
    far_cross = e == -d
    is_cross = e != 0
    is_relay = (u == 0) | (u == 7)
    has_back = (t - e >= 0) & (t - e < GT)
    has_ahead = (t + e >= 0) & (t + e < GT)
    mine = pl.multiple_of(p * HALF, 128)
    theirs = pl.multiple_of((1 - p) * HALF, 128)
    scale = HD ** (-0.5)

    @pl.when(jnp.logical_not(has_down))
    def _():
        for s in (0, 3, 6, 9):
            kv[:, pl.ds(s * T, T), :] = jnp.zeros((NH, T, 2 * HD), BF)
        rz[:, 1] = jnp.zeros((NH, 2 * T, 2 * HD), BF)

    @pl.when(jnp.logical_not(has_up))
    def _():
        for s in (2, 5, 8, 11):
            kv[:, pl.ds(s * T, T), :] = jnp.zeros((NH, T, 2 * HD), BF)
        rz[:, 0] = jnp.zeros((NH, 2 * T, 2 * HD), BF)

    for n, side, there, crossing in ((0, 0, has_near, near_cross), (1, 3, has_far, far_cross)):
        @pl.when(jnp.logical_not(there))
        def _():
            kv[:, pl.ds(side * SIDE, SIDE), :] = jnp.zeros((NH, SIDE, 2 * HD), BF)

        @pl.when(jnp.logical_not(there) | crossing)
        def _():
            rx[:, n] = jnp.zeros((NH, SIDE, 2 * HD), BF)

    barrier = pltpu.get_barrier_semaphore()
    greeted = 0
    for peer, cond in (
        (partner, None), (sibling, None), (across, None), (near, has_near), (far, has_far), (up, has_up),
        (down, has_down), (eight_off, is_cross | is_relay), (six_off, is_relay),
        (relay, is_cross), (back, is_cross & has_back),
    ):
        if cond is None:
            pl.semaphore_signal(barrier, inc=1, device_id=peer, device_id_type=MESH)
            greeted += 1
        else:
            @pl.when(cond)
            def _():
                pl.semaphore_signal(barrier, inc=1, device_id=peer, device_id_type=MESH)
            greeted += cond.astype(jnp.int32)

    pending = []

    def when(cond, action):
        if cond is None:
            action()
        else:
            @pl.when(cond)
            def _():
                action()

    def local(src, dst, n):
        copy = pltpu.make_async_copy(src, dst, lsem.at[n])
        copy.start()
        return copy

    def remote(src, dst, send, recv, device, cond=None):
        copy = pltpu.make_async_remote_copy(
            src_ref=src, dst_ref=dst, send_sem=send, recv_sem=recv, device_id=device, device_id_type=MESH
        )
        when(cond, copy.start)
        pending.append((cond, copy))

    def arrived(dst, recv, cond=None):
        copy = pltpu.make_async_remote_copy(
            src_ref=dst, dst_ref=dst, send_sem=lsem.at[0], recv_sem=recv, device_id=partner, device_id_type=MESH
        )
        when(cond, copy.wait_recv)

    def slot(h, s):
        return kv.at[h, pl.ds(s * T, T), :]

    g_copy = local(g_in, gall.at[0], 13)
    out_copies = []
    own_copies = []
    for h in range(NH):
        there = pl.multiple_of(theirs + h * HD, 128)
        here = pl.multiple_of(mine + h * HD, 128)
        out_copies.append((
            local(k_in.at[:, pl.ds(there, HD)], kvo.at[h, :, pl.ds(0, HD)], 4 * h),
            local(v_in.at[:, pl.ds(there, HD)], kvo.at[h, :, pl.ds(HD, HD)], 4 * h + 1),
        ))
        own_copies.append((
            local(k_in.at[:, pl.ds(here, HD)], kv.at[h, pl.ds(4 * T, T), pl.ds(0, HD)], 4 * h + 2),
            local(v_in.at[:, pl.ds(here, HD)], kv.at[h, pl.ds(4 * T, T), pl.ds(HD, HD)], 4 * h + 3),
        ))
    q_copy = local(q_in.at[:, pl.ds(mine, HALF)], qb.at[0], 12)
    qo_copy = local(q_in.at[:, pl.ds(theirs, HALF)], qo, 16)
    wo_copy = local(w_in.at[:, pl.ds(theirs, HALF)], wo, 14)
    wm_copy = local(w_in.at[:, pl.ds(mine, HALF)], wm, 15)

    lanes = lax.broadcasted_iota(jnp.int32, (1, WIN), 1)
    for a in range(2):
        row = jnp.zeros((1, WIN), F32)
        for n in range(9):
            g_slot, t_slot = a + n // 3, n % 3
            t_abs = t + t_slot - 1
            g_abs = g + (g_slot - 1) * (1 - 2 * p)
            if t_slot == 1 and g_slot == a + 1:
                value = jnp.float32(0.0)
            else:
                flag = valid[((t_abs + GT) % GT) * GH + (g_abs + GH) % GH]
                inside = (t_abs >= 0) & (t_abs < GT) & (g_abs >= 0) & (g_abs < GH)
                value = jnp.where(inside & (flag > 0), 0.0, -jnp.inf).astype(F32)
            row = jnp.where((lanes >= n * T) & (lanes < (n + 1) * T), value, row)
        bias[a] = row

    pl.semaphore_wait(barrier, greeted)

    def send_side(h, s, target, n, device, there, crossing):
        tile = slot(h, s)
        remote(tile, slot(h, target), fs.at[h, n], fr.at[h, target], device, there & jnp.logical_not(crossing))
        remote(tile, rb.at[h], rls.at[h, 0], rlr.at[h, 0], relay, crossing)
        remote(
            tile, slot(h, target + e), fs.at[h, n + 1], fr.at[h, target + e], back, crossing & has_back
        )

    def send_own(h):
        for copy in own_copies[h]:
            copy.wait()
        own = slot(h, 4)
        remote(own, slot(h, 3), fs.at[h, 0], fr.at[h, 3], up, has_up)
        remote(own, slot(h, 5), fs.at[h, 1], fr.at[h, 5], down, has_down)
        send_side(h, 4, 10, 2, near, has_near, near_cross)

    def send_other(h):
        arrived(slot(h, 7), fr.at[h, 7])
        other = slot(h, 7)
        remote(other, slot(h, 6), fs.at[h, 4], fr.at[h, 6], up, has_up)
        remote(other, slot(h, 8), fs.at[h, 5], fr.at[h, 8], down, has_down)
        send_side(h, 7, 1, 6, far, has_far, far_cross)

    def pass_on(h):
        arrived(rb.at[h], rlr.at[h, 0], is_relay)
        target = jnp.where((u == 0) == (p == 1), 10, 1)
        remote(rb.at[h], slot(h, target), rls.at[h, 1], fr.at[h, target], relay_to, is_relay)

    def forward(h):
        for n, (s, target, device, there, crossing, exists, way) in enumerate((
            (3, 9, near, has_near, near_cross, has_down, 1),
            (5, 11, near, has_near, near_cross, has_up, -1),
            (6, 0, far, has_far, far_cross, has_down, 1),
            (8, 2, far, has_far, far_cross, has_up, -1),
        )):
            arrived(slot(h, s), fr.at[h, s], exists)
            remote(
                slot(h, s), slot(h, target), fs.at[h, 8 + n], fr.at[h, target], device,
                exists & there & (jnp.logical_not(crossing) | (e == way)),
            )

    def cols(h):
        return pl.ds(h * HD, HD)

    def send_back(h, n, device, there, crossing):
        remote(
            xs.at[h, n], rx.at[h, n], bxs.at[h, n, 0], bxr.at[h, n, 0], device, there & jnp.logical_not(crossing)
        )
        remote(xs.at[h, n, pl.ds(T, T)], rb2.at[h], rls.at[h, 2], rlr.at[h, 1], relay, crossing)
        rows = pl.ds((1 + e) * T, T)
        remote(
            xs.at[h, n, rows], rx.at[h, n, rows], bxs.at[h, n, 1], bxr.at[h, n, 2], device, crossing & has_ahead
        )
        remote(xs.at[h, n, pl.ds((1 - e) * T, T)], rc.at[h], bcs.at[h, n], bcr.at[h], back, crossing & has_back)

    def pass_back(h):
        arrived(rb2.at[h], rlr.at[h, 1], is_relay)
        n = jnp.where(u == 0, p, 1 - p)
        remote(rb2.at[h], rx.at[h, n, pl.ds(T, T)], rls.at[h, 3], bxr.at[h, n, 1], relay_to, is_relay)

    def attend(h):
        for s, there in ((9, has_far & has_down), (10, has_far), (11, has_far & has_up),
                         (0, has_near & has_down), (1, has_near), (2, has_near & has_up)):
            arrived(slot(h, s), fr.at[h, s], there)
        for a in range(2):
            window = pl.ds(a * SIDE, WIN)
            s = nt(qb[a, :, cols(h)], kv[h, window, pl.ds(0, HD)]) * scale + bias[a]
            x = jnp.exp(s - jnp.max(s, axis=1, keepdims=True))
            weights = (x * (1.0 / jnp.sum(x, axis=1, keepdims=True))).astype(BF)
            pb[a] = weights
            att[a, :, cols(h)] = nn(weights, kv[h, window, pl.ds(HD, HD)]).astype(BF)
        remote(att.at[1, :, cols(h)], attr.at[:, cols(h)], ats.at[h], atr.at[h], partner)

    def differentiate(h):
        for a in range(2):
            q = qb[a, :, cols(h)]
            do = dob[a, :, cols(h)]
            window = pl.ds(a * SIDE, WIN)
            k = kv[h, window, pl.ds(0, HD)]
            weights = pb[a]
            row_dot = jnp.sum(do.astype(F32) * att[a, :, cols(h)].astype(F32), axis=1, keepdims=True)
            weight_grad = nt(do, kv[h, window, pl.ds(HD, HD)])
            score_grad = (weights.astype(F32) * (weight_grad - row_dot) * scale).astype(BF)
            dqb[a, :, cols(h)] = nn(score_grad, k).astype(BF)
            for part, lhs, rhs in ((0, score_grad, q), (1, weights, do)):
                grad = tn(lhs, rhs)
                lane = pl.ds(part * HD, HD)
                if a == 0:
                    xs[h, 1, :, lane] = grad[:SIDE].astype(BF)
                    acc[h, :, lane] = grad[SIDE:]
                else:
                    acc[h, :, lane] += grad[:2 * SIDE]
                    xs[h, 0, :, lane] = grad[2 * SIDE:].astype(BF)
            if a == 0:
                send_back(h, 1, near, has_near, near_cross)
            else:
                send_back(h, 0, far, has_far, far_cross)
        here = pl.multiple_of(mine + h * HD, 128)
        remote(dqb.at[1, :, cols(h)], dq_out.at[:, pl.ds(here, HD)], qs.at[1 + h], qr.at[1 + h], partner)

    def reduce_x(h):
        pass_back(h)
        for n, there, crossing in ((0, has_near, near_cross), (1, has_far, far_cross)):
            arrived(rx.at[h, n], bxr.at[h, n, 0], there & jnp.logical_not(crossing))
            arrived(rx.at[h, n, pl.ds(T, T)], bxr.at[h, n, 1], crossing)
            arrived(rx.at[h, n, pl.ds((1 - e) * T, T)], bxr.at[h, n, 2], crossing & has_back)
            for part, row in ((0, 0), (1, 2 * T)):
                zs[h, part, pl.ds(n * T, T), :] = (
                    acc[h, pl.ds(n * SIDE + row, T), :] + rx[h, n, pl.ds(row, T), :].astype(F32)
                ).astype(BF)
            acc[h, pl.ds(n * SIDE + T, T), :] += rx[h, n, pl.ds(T, T), :].astype(F32)
        remote(zs.at[h, 0], rz.at[h, 0], bzs.at[h, 0], bzr.at[h, 0], down, has_down)
        remote(zs.at[h, 1], rz.at[h, 1], bzs.at[h, 1], bzr.at[h, 1], up, has_up)

    def reduce_z(h):
        arrived(rz.at[h, 0], bzr.at[h, 0], has_up)
        arrived(rz.at[h, 1], bzr.at[h, 1], has_down)
        arrived(rc.at[h], bcr.at[h], is_cross & has_back)
        for n, crossing in ((0, near_cross), (1, far_cross)):
            @pl.when(crossing & has_back)
            def _():
                acc[h, pl.ds(n * SIDE + T, T), :] += rc[h].astype(F32)

        for n, out in ((1, ys), (0, yo)):
            rows = pl.ds(n * T, T)
            out[h] = (
                acc[h, pl.ds(n * SIDE + T, T), :] + rz[h, 0, rows, :].astype(F32) + rz[h, 1, rows, :].astype(F32)
            ).astype(BF)
        here = pl.ds(pl.multiple_of(mine + h * HD, 128), HD)
        for part, out in ((0, dk_out), (1, dv_out)):
            lane = pl.ds(part * HD, HD)
            remote(ys.at[h, :, lane], out.at[:, here], bys.at[h, part], byr.at[h, part], partner)
            finals.append(local(yo.at[h, :, lane], out.at[:, here], 20 + 2 * h + part))

    finals = []

    g_copy.wait()
    remote(gall.at[0], gall.at[2], gs.at[1], gr.at[1], across)
    remote(gall.at[0], gall.at[1], gs.at[0], gr.at[0], sibling)
    for h in range(NH):
        for copy in out_copies[h]:
            copy.wait()
        remote(kvo.at[h], slot(h, 7), fs.at[h, 12], fr.at[h, 7], partner)
        if h < 2:
            send_own(h)
    qo_copy.wait()
    remote(qo, qb.at[1], qs.at[0], qr.at[0], partner)
    arrived(gall.at[2], gr.at[1])
    remote(gall.at[2], gall.at[3], gs.at[2], gr.at[2], sibling)
    send_other(0)
    send_own(2)
    pass_on(0)

    wo_copy.wait()
    wm_copy.wait()
    arrived(gall.at[1], gr.at[0])
    arrived(gall.at[3], gr.at[2])
    blocks = (j, j1, j2, j3)
    rows = [pl.ds(pl.multiple_of(block * FULL, FULL), FULL) for block in blocks]
    total = nn(gall[0], wo[rows[0], :])
    for n in range(1, 4):
        total = total + nn(gall[n], wo[rows[n], :])
    dop[...] = total.astype(BF)
    remote(dop, dob.at[1], qs.at[4], qr.at[4], partner)
    send_other(1)
    pass_on(1)
    total = nn(gall[0], wm[rows[0], :])
    for n in range(1, 4):
        total = total + nn(gall[n], wm[rows[n], :])
    dob[0] = total.astype(BF)
    forward(0)
    send_other(2)
    pass_on(2)
    q_copy.wait()
    arrived(qb.at[1], qr.at[0])

    forward(1)
    attend(0)
    arrived(dob.at[1], qr.at[4])
    differentiate(0)
    forward(2)
    attend(1)
    differentiate(1)
    reduce_x(0)
    attend(2)
    differentiate(2)
    finals.append(local(dqb.at[0], dq_out.at[:, pl.ds(mine, HALF)], 26))
    reduce_x(1)
    reduce_z(0)

    for h in range(NH):
        arrived(attr.at[:, cols(h)], atr.at[h])

    def project(n):
        return nt(att[0], wm[rows[n], :]) + nt(attr[...], wo[rows[n], :])

    ms[0] = project(3).astype(BF)
    ms[1] = project(1).astype(BF)
    remote(ms, mr, mss.at[0], msr.at[0], sibling)
    reduce_x(2)
    crossing = project(2)
    arrived(mr, msr.at[0])
    ms2[...] = (crossing + mr[0].astype(F32)).astype(BF)
    remote(ms2, mr2, mss.at[1], msr.at[1], across)
    kept = project(0) + mr[1].astype(F32)
    reduce_z(1)
    arrived(mr2, msr.at[1])
    mo[...] = (kept + mr2[...].astype(F32)).astype(BF)
    finals.append(local(mo, mixed, 27))
    reduce_z(2)

    for h in range(NH):
        there = pl.ds(pl.multiple_of(theirs + h * HD, 128), HD)
        arrived(dq_out.at[:, there], qr.at[1 + h])
        arrived(dk_out.at[:, there], byr.at[h, 0])
        arrived(dv_out.at[:, there], byr.at[h, 1])
    for copy in finals:
        copy.wait()
    for cond, copy in pending:
        when(cond, copy.wait_send)


def hand_over(*refs):
    for n in range(4):
        refs[4 + n][...] = refs[n][...]


def on_device(queries, keys, values, w_out, out_grad, tile_valid):
    dma = pltpu.SemaphoreType.DMA
    any_space = pl.BlockSpec(memory_space=pl.ANY)
    block = jax.ShapeDtypeStruct(queries.shape, BF)
    results = pl.pallas_call(
        kernel,
        out_shape=(block, block, block, block),
        in_specs=[any_space] * 5 + [pl.BlockSpec(memory_space=pltpu.SMEM)],
        out_specs=(any_space, any_space, any_space, any_space),
        scratch_shapes=[
            pltpu.VMEM((NH, 12 * T, 2 * HD), BF),
            pltpu.VMEM((NH, T, 2 * HD), BF),
            pltpu.VMEM((2, T, HALF), BF),
            pltpu.VMEM((2, T, HALF), BF),
            pltpu.VMEM((T, HALF), BF),
            pltpu.VMEM((4, T, FULL), BF),
            pltpu.VMEM((4 * FULL, HALF), BF),
            pltpu.VMEM((4 * FULL, HALF), BF),
            pltpu.VMEM((2, T, HALF), BF),
            pltpu.VMEM((T, HALF), BF),
            pltpu.VMEM((2, T, HALF), BF),
            pltpu.VMEM((2, 1, WIN), F32),
            pltpu.VMEM((NH, 2, SIDE, 2 * HD), BF),
            pltpu.VMEM((NH, 2, SIDE, 2 * HD), BF),
            pltpu.VMEM((NH, 2 * SIDE, 2 * HD), F32),
            pltpu.VMEM((NH, 2, 2 * T, 2 * HD), BF),
            pltpu.VMEM((NH, 2, 2 * T, 2 * HD), BF),
            pltpu.VMEM((NH, T, 2 * HD), BF),
            pltpu.VMEM((NH, T, 2 * HD), BF),
            pltpu.VMEM((2, T, FULL), BF),
            pltpu.VMEM((2, T, FULL), BF),
            pltpu.VMEM((T, FULL), BF),
            pltpu.VMEM((T, FULL), BF),
            pltpu.VMEM((T, FULL), BF),
            pltpu.VMEM((NH, T, 2 * HD), BF),
            pltpu.VMEM((NH, T, 2 * HD), BF),
            pltpu.VMEM((NH, T, 2 * HD), BF),
            pltpu.VMEM((2, T, WIN), BF),
            pltpu.VMEM((T, HALF), BF),
            dma((28,)),
            dma((NH, 13)),
            dma((NH, 12)),
            dma((NH, 2, 2)),
            dma((NH, 2, 3)),
            dma((NH, 2)),
            dma((NH, 2)),
            dma((NH, 2)),
            dma((NH, 2)),
            dma((3,)),
            dma((3,)),
            dma((5,)),
            dma((5,)),
            dma((NH,)),
            dma((NH,)),
            dma((2,)),
            dma((2,)),
            dma((NH, 4)),
            dma((NH, 2)),
            dma((NH, 2)),
            dma((NH,)),
        ],
        compiler_params=pltpu.CompilerParams(
            collective_id=0, has_side_effects=True, vmem_limit_bytes=56 * 1024 * 1024
        ),
    )(queries, keys, values, w_out, out_grad, tile_valid)
    whole = pl.BlockSpec(memory_space=pltpu.VMEM)
    return pl.pallas_call(
        hand_over,
        out_shape=(block, block, block, block),
        in_specs=[whole] * 4,
        out_specs=(whole, whole, whole, whole),
    )(*results)


def solution(mesh):
    return jax.shard_map(
        on_device,
        mesh=mesh,
        in_specs=(
            P("tile", "head"),
            P("tile", "head"),
            P("tile", "head"),
            P(None, "head"),
            P("tile", "head"),
            P(),
        ),
        out_specs=(P("tile", "head"), P("tile", "head"), P("tile", "head"), P("tile", "head")),
        check_vma=False,
    )
```

time: 94.6 us -> 80.8 us (0.85)
  Pallas kernels: 93.8 us -> 79.8 us
    pallas_call x1, Pallas kernels: 91.5 us -> 77.5 us  [on_device(): pl.pallas_call(kernel, out_shape=(block, block, block, block), in_specs=[...]
where the time goes in v3:
time: 80.8 us; the launch traced here: 80.4 us
  Pallas kernels  79.8 us (99%)
    pallas_call x1, Pallas kernels, on_device(): pl.pallas_call(kernel, out_shape=(block, block, block, block), in_specs=[...  77.5 us
    pallas_call x1, Pallas kernels, on_device(): pl.pallas_call(hand_over, out_shape=(block, block, block, block), in_spec...  2.27 us

profile of v3, /device:TPU:32, one launch (start us, length us, event | category | flops | bytes accessed | tf_op | source)
XLA Modules:
  0.0 80.4 jit_solution(4334004456504740031)
XLA Ops:
  0.6 77.5 %shard_map.93 = (bf16[160,768]{1,0:T(8,128)(2,1)}, bf16[160,768]{1,0:T(8,128)(2,1)}, bf16[160,768]{1,0:T(8,128)(2,1)}, bf16[160,768]{1,0:T(8,128)(2,1)}) custom-call(bf16[160,768]{1,0:T(8,128)(2,1)} %q_in.1, bf16[160,768]{1,0:T(8,128)(2,1)} %k_in.1, bf16[160,768]{1,0:T(8,128)(2,1)} %v_in.1, bf16[3072,768]{1,0:T(8,128)(2,1)} %w_in.1, bf16[160,768]{1,0:T(8,128)(2,1)} %g_in.1, ...), custom_call_target="tpu_custom_call" | custom-call | tf_op jit(solution)/shard_map/pallas_call | solution.py:414
  78.2 2.3 %shard_map.94 = (bf16[160,768]{1,0:T(8,128)(2,1)}, bf16[160,768]{1,0:T(8,128)(2,1)}, bf16[160,768]{1,0:T(8,128)(2,1)}, bf16[160,768]{1,0:T(8,128)(2,1)}) custom-call(bf16[160,768]{1,0:T(8,128)(2,1)} %get-tuple-element.8.refs_0_, bf16[160,768]{1,0:T(8,128)(2,1)} %get-tuple-element.9.refs_1_, bf16[160,768]{1,0:T(8,128)(2,1)} %get-tuple-element.10.refs_2_, ...), custom_call_target="tpu_custom_call" | custom-call | tf_op jit(solution)/shard_map/pallas_call | solution.py:476

commit v4 on v2

--- a/solution.py
+++ b/solution.py
@@ -46,16 +46,18 @@
     u = g // 2
     d = 2 * p - 1
     e = (u == 3).astype(jnp.int32) - (u == 4).astype(jnp.int32)
+    partner = (i + 1 - 2 * p, j)
     near = (t * GH + (g + 2 * d + GH) % GH, j)
     far = (t * GH + (g - 2 * d + GH) % GH, j)
     up = (((t + 1) % GT) * GH + g, j)
     down = (((t + GT - 1) % GT) * GH + g, j)
-    relay = (t * GH + (g + GH // 2) % GH, j)
-    relay_to = (t * GH + (g + 6 + 4 * (u == 7).astype(jnp.int32)) % GH, j)
+    eight_off = (t * GH + (g + GH // 2) % GH, j)
+    six_off = (t * GH + (g + 6 + 4 * (u == 7).astype(jnp.int32)) % GH, j)
+    relay = (t * GH + (g + GH - 6 * e) % GH, j)
+    relay_to = eight_off
     back = (((t - e + GT) % GT) * GH + (g + 2 * e), j)
     j1 = j + 1 - 2 * (j % 2)
     j2 = (j + 2) % 4
-    partner = (i + 1 - 2 * p, j2)
     j3 = (j1 + 2) % 4
     sibling = (i, j1)
     across = (i, j2)
@@ -98,8 +100,8 @@
     greeted = 0
     for peer, cond in (
         (partner, None), (sibling, None), (across, None), (near, has_near), (far, has_far), (up, has_up),
-        (down, has_down), (relay, is_cross | is_relay), (relay_to, is_relay),
-        ((t * GH + (g + GH - 6 * e) % GH, j), is_cross), (back, is_cross & has_back),
+        (down, has_down), (eight_off, is_cross | is_relay), (six_off, is_relay),
+        (relay, is_cross), (back, is_cross & has_back),
     ):
         if cond is None:
             pl.semaphore_signal(barrier, inc=1, device_id=peer, device_id_type=MESH)
@@ -151,17 +153,21 @@
 
     staged = [
         [
-            local(source.at[:, columns(h)], kvo.at[h, n, :, pl.ds(part * HD, HD)], hsem.at[h, 2 * n + part])
-            for n, columns in enumerate((mine_cols, their_cols))
-            for part, source in enumerate((k_in, v_in))
+            local(k_in.at[:, their_cols(h)], kvo.at[h, :, pl.ds(0, HD)], hsem.at[h, 0]),
+            local(v_in.at[:, their_cols(h)], kvo.at[h, :, pl.ds(HD, HD)], hsem.at[h, 1]),
+        ]
+        for h in range(NH)
+    ]
+    kept_tiles = [
+        [
+            local(k_in.at[:, mine_cols(h)], slot(h, 4).at[:, pl.ds(0, HD)], hsem.at[h, 2]),
+            local(v_in.at[:, mine_cols(h)], slot(h, 4).at[:, pl.ds(HD, HD)], hsem.at[h, 3]),
         ]
         for h in range(NH)
     ]
     g_copy = local(g_in, gall.at[0], lsem.at[0])
-    q_copies = [
-        local(q_in.at[:, pl.ds(mine, HALF)], qo.at[0], lsem.at[1]),
-        local(q_in.at[:, pl.ds(theirs, HALF)], qo.at[1], lsem.at[2]),
-    ]
+    q_copy = local(q_in.at[:, pl.ds(mine, HALF)], qb.at[0], lsem.at[1])
+    qo_copy = local(q_in.at[:, pl.ds(theirs, HALF)], qo, lsem.at[2])
     w_copies = [
         local(w_in.at[:, pl.ds(theirs, HALF)], wo, lsem.at[3]),
         local(w_in.at[:, pl.ds(mine, HALF)], wm, lsem.at[4]),
@@ -194,8 +200,7 @@
         )
 
     def send_swap(act, h):
-        remote(act, kvo.at[h, 0], slot(h, 4), fs.at[h, 12], fr.at[h, 4], across)
-        remote(act, kvo.at[h, 1], slot(h, 7), fs.at[h, 13], fr.at[h, 7], partner)
+        remote(act, kvo.at[h], slot(h, 7), fs.at[h, 12], fr.at[h, 7], partner)
 
     def send_z(act, h, s):
         remote(act, slot(h, s), slot(h, s - 1), fs.at[h, 0 if s == 4 else 2], fr.at[h, s - 1], up, has_up)
@@ -208,19 +213,19 @@
         send_side(act, h, 7, 1, 6, far, has_far, far_cross)
 
     def pass_on(act, h):
-        target = jnp.where((u == 7) == (p == 1), 10, 1)
+        target = jnp.where((u == 0) == (p == 1), 10, 1)
         remote(act, rb.at[h], slot(h, target), rls.at[h, 1], fr.at[h, target], relay_to, is_relay)
 
-    def forward(act, h, n):
+    def forward(act, h, n, k):
         target, device, there, crossing = ((9, near, has_near, near_cross), (0, far, has_far, far_cross))[n]
-        for k, exists, way in ((0, has_down, 1), (2, has_up, -1)):
-            source = slot(h, 3 + 3 * n + k)
-            if act == START:
-                arrived(source, fr.at[h, 3 + 3 * n + k], exists)
-            remote(
-                act, source, slot(h, target + k), fs.at[h, 8 + 2 * n + k // 2], fr.at[h, target + k], device,
-                exists & there & (jnp.logical_not(crossing) | (e == way)),
-            )
+        exists, way = ((has_down, 1), (has_up, -1))[k]
+        source = slot(h, 3 + 3 * n + 2 * k)
+        if act == START:
+            arrived(source, fr.at[h, 3 + 3 * n + 2 * k], exists)
+        remote(
+            act, source, slot(h, target + 2 * k), fs.at[h, 8 + 2 * n + k], fr.at[h, target + 2 * k], device,
+            exists & there & (jnp.logical_not(crossing) | (e == way)),
+        )
 
     def send_back(act, h, n):
         device, there, crossing = ((far, has_far, far_cross), (near, has_near, near_cross))[n]
@@ -238,28 +243,33 @@
         )
 
     def pass_back(act, h):
-        n = jnp.where(u == 7, p, 1 - p)
+        n = jnp.where(u == 0, p, 1 - p)
         remote(act, rb2.at[h], rx.at[h, n, pl.ds(T, T)], rls.at[h, 3], bxr.at[h, n, 1], relay_to, is_relay)
 
     def send_attended(act, h):
-        for n, device in enumerate((across, partner)):
-            remote(act, att.at[n, :, cols(h)], attr.at[n, :, cols(h)], ats.at[h, n], atr.at[h, n], device)
+        remote(act, att.at[1, :, cols(h)], attr.at[:, cols(h)], ats.at[h], atr.at[h], partner)
 
     def send_query_grad(act, h):
-        for n, device in enumerate((across, partner)):
-            remote(act, dqb.at[n, :, cols(h)], dq_out.at[:, mine_cols(h)], dqs.at[h, n], dqr.at[h, n], device)
+        remote(act, dqb.at[1, :, cols(h)], dq_out.at[:, mine_cols(h)], dqs.at[h], dqr.at[h], partner)
+        copy = pltpu.make_async_copy(dqb.at[0, :, cols(h)], dq_out.at[:, mine_cols(h)], hsem.at[h, 2])
+        if act == START:
+            copy.start()
+        else:
+            copy.wait()
 
     def send_reduced(act, h):
         remote(act, zs.at[h, 0], rz.at[h, 0], bzs.at[h, 0], bzr.at[h, 0], down, has_down)
         remote(act, zs.at[h, 1], rz.at[h, 1], bzs.at[h, 1], bzr.at[h, 1], up, has_up)
 
     def send_total(act, h):
-        for n, device in enumerate((across, partner)):
-            for part, out in enumerate((dk_out, dv_out)):
-                remote(
-                    act, ys.at[h, n, :, pl.ds(part * HD, HD)], out.at[:, mine_cols(h)], bys.at[h, n, part],
-                    byr.at[h, n, part], device,
-                )
+        for part, out in enumerate((dk_out, dv_out)):
+            lane = pl.ds(part * HD, HD)
+            remote(act, ys.at[h, 1, :, lane], out.at[:, mine_cols(h)], bys.at[h, part], byr.at[h, part], partner)
+            copy = pltpu.make_async_copy(ys.at[h, 0, :, lane], out.at[:, mine_cols(h)], hsem.at[h, part])
+            if act == START:
+                copy.start()
+            else:
+                copy.wait()
 
     def attend(h):
         for s, there in ((9, has_far & has_down), (10, has_far), (11, has_far & has_up),
@@ -343,112 +353,119 @@
         remote(act, gall.at[source], gall.at[target], gs.at[k], gr.at[k], device)
 
     def send_queries(act):
-        for n, device in enumerate((across, partner)):
-            remote(act, qo.at[n], qb.at[n], qs.at[n], qr.at[n], device)
-
-    def send_attn_grad(n):
-        weights_ref = (wm, wo)[n]
+        remote(act, qo, qb.at[1], qs.at[0], qr.at[0], partner)
+
+    def attn_grad(weights_ref):
         total = nn(gall[0], weights_ref[rows[0], :])
         for k in range(1, 4):
             total = total + nn(gall[k], weights_ref[rows[k], :])
-        dop[n] = total.astype(BF)
-        remote(START, dop.at[n], dob.at[n], qs.at[2 + n], qr.at[2 + n], (across, partner)[n])
+        return total.astype(BF)
+
+    def send_attn_grad(act):
+        remote(act, dop, dob.at[1], qs.at[1], qr.at[1], partner)
 
     def project(n):
-        return nt(attr[0], wm[rows[n], :]) + nt(attr[1], wo[rows[n], :])
-
+        return nt(att[0], wm[rows[n], :]) + nt(attr[...], wo[rows[n], :])
+
+    for copy in staged[0]:
+        copy.wait()
+    send_swap(START, 0)
+    for copy in kept_tiles[0]:
+        copy.wait()
+    send_z(START, 0, 4)
+    for copy in staged[1]:
+        copy.wait()
+    send_swap(START, 1)
+    arrived(slot(0, 7), fr.at[0, 7])
+    send_z(START, 0, 7)
+    for copy in kept_tiles[1]:
+        copy.wait()
+    send_z(START, 1, 4)
     g_copy.wait()
     send_gathered(START, 0)
-    send_gathered(START, 1)
-    for copy in staged[0]:
-        copy.wait()
-    send_swap(START, 0)
-    for copy in staged[1]:
-        copy.wait()
-    send_swap(START, 1)
-    for copy in staged[2]:
-        copy.wait()
-    send_swap(START, 2)
-    arrived(slot(0, 4), fr.at[0, 4])
-    send_z(START, 0, 4)
     send_own_x(START, 0)
-    arrived(slot(0, 7), fr.at[0, 7])
-    send_z(START, 0, 7)
-    send_other_x(START, 0)
-    arrived(slot(1, 4), fr.at[1, 4])
-    send_z(START, 1, 4)
-    send_own_x(START, 1)
-    for copy in q_copies:
-        copy.wait()
-    send_queries(START)
     arrived(gall.at[2], gr.at[1])
     send_gathered(START, 2)
     arrived(slot(1, 7), fr.at[1, 7])
     send_z(START, 1, 7)
-    send_other_x(START, 1)
-    arrived(slot(2, 4), fr.at[2, 4])
-    send_z(START, 2, 4)
-    send_own_x(START, 2)
+    forward(START, 0, 1, 0)
+    for copy in staged[2]:
+        copy.wait()
+    send_swap(START, 2)
+    forward(START, 0, 0, 0)
+    send_gathered(START, 1)
     arrived(rb.at[0], rlr.at[0, 0], is_relay)
     pass_on(START, 0)
+    forward(START, 0, 0, 1)
+    send_other_x(START, 0)
+    qo_copy.wait()
+    send_queries(START)
+    forward(START, 0, 1, 1)
+    send_own_x(START, 1)
+    forward(START, 1, 0, 0)
     for copy in w_copies:
         copy.wait()
     arrived(gall.at[1], gr.at[0])
     arrived(gall.at[3], gr.at[2])
-    send_attn_grad(1)
-    send_attn_grad(0)
+    dop[...] = attn_grad(wo)
+    send_attn_grad(START)
+    dob[0] = attn_grad(wm)
     arrived(slot(2, 7), fr.at[2, 7])
     send_z(START, 2, 7)
-    send_other_x(START, 2)
+    for copy in kept_tiles[2]:
+        copy.wait()
+    send_z(START, 2, 4)
     arrived(rb.at[1], rlr.at[1, 0], is_relay)
     pass_on(START, 1)
-    forward(START, 0, 0)
-    forward(START, 0, 1)
+    send_other_x(START, 1)
+    send_own_x(START, 2)
+    forward(START, 1, 0, 1)
+    send_other_x(START, 2)
+    q_copy.wait()
+    arrived(qb.at[1], qr.at[0])
+    attend(0)
+    forward(START, 1, 1, 1)
+    forward(START, 1, 1, 0)
+    arrived(dob.at[1], qr.at[1])
+    differentiate(0, 0)
+    differentiate(0, 1)
+    forward(START, 2, 0, 0)
+    arrived(rb2.at[0], rlr.at[0, 1], is_relay)
+    pass_back(START, 0)
+    forward(START, 2, 1, 0)
+    attend(1)
     arrived(rb.at[2], rlr.at[2, 0], is_relay)
     pass_on(START, 2)
-    forward(START, 1, 0)
-    forward(START, 1, 1)
-    for n in range(2):
-        arrived(qb.at[n], qr.at[n])
-    attend(0)
-    for n in range(2):
-        arrived(dob.at[n], qr.at[2 + n])
-    differentiate(0, 0)
-    differentiate(0, 1)
-    forward(START, 2, 0)
-    forward(START, 2, 1)
-    attend(1)
+    forward(START, 2, 0, 1)
+    forward(START, 2, 1, 1)
     differentiate(1, 0)
     differentiate(1, 1)
-    arrived(rb2.at[0], rlr.at[0, 1], is_relay)
-    pass_back(START, 0)
     reduce_x(0)
+    arrived(rb2.at[1], rlr.at[1, 1], is_relay)
+    pass_back(START, 1)
     attend(2)
     differentiate(2, 0)
     differentiate(2, 1)
-    arrived(rb2.at[1], rlr.at[1, 1], is_relay)
-    pass_back(START, 1)
     reduce_x(1)
-    reduce_z(0)
+    arrived(rb2.at[2], rlr.at[2, 1], is_relay)
+    pass_back(START, 2)
     for h in range(NH):
-        for n in range(2):
-            arrived(attr.at[n, :, cols(h)], atr.at[h, n])
+        arrived(attr.at[:, cols(h)], atr.at[h])
     ms[0] = project(3).astype(BF)
     ms[1] = project(1).astype(BF)
     remote(START, ms, mr, mss.at[0], msr.at[0], sibling)
-    arrived(rb2.at[2], rlr.at[2, 1], is_relay)
-    pass_back(START, 2)
-    reduce_x(2)
     crossing_sum = project(2)
     arrived(mr, msr.at[0])
     ms2[...] = (crossing_sum + mr[0].astype(F32)).astype(BF)
     remote(START, ms2, mr2, mss.at[1], msr.at[1], across)
     kept = project(0) + mr[1].astype(F32)
+    reduce_x(2)
+    reduce_z(0)
     reduce_z(1)
+    reduce_z(2)
     arrived(mr2, msr.at[1])
     mo[...] = (kept + mr2[...].astype(F32)).astype(BF)
     mixed_copy = local(mo, mixed, lsem.at[5])
-    reduce_z(2)
     send_z(WAIT, 0, 4)
     send_z(WAIT, 0, 7)
     send_z(WAIT, 1, 4)
@@ -459,8 +476,7 @@
     for n in range(3):
         send_gathered(WAIT, n)
     send_queries(WAIT)
-    for n, device in enumerate((across, partner)):
-        remote(WAIT, dop.at[n], dob.at[n], qs.at[2 + n], qr.at[2 + n], device)
+    send_attn_grad(WAIT)
     remote(WAIT, ms, mr, mss.at[0], msr.at[0], sibling)
     remote(WAIT, ms2, mr2, mss.at[1], msr.at[1], across)
     for h in range(NH):
@@ -469,12 +485,13 @@
             send_total,
         ):
             send(WAIT, h)
-        for n, columns in enumerate((mine_cols, their_cols)):
-            forward(WAIT, h, n)
+        for n in range(2):
+            forward(WAIT, h, n, 0)
+            forward(WAIT, h, n, 1)
             send_back(WAIT, h, n)
-            arrived(dq_out.at[:, columns(h)], dqr.at[h, n])
-            arrived(dk_out.at[:, columns(h)], byr.at[h, n, 0])
-            arrived(dv_out.at[:, columns(h)], byr.at[h, n, 1])
+        arrived(dq_out.at[:, their_cols(h)], dqr.at[h])
+        arrived(dk_out.at[:, their_cols(h)], byr.at[h, 0])
+        arrived(dv_out.at[:, their_cols(h)], byr.at[h, 1])
     mixed_copy.wait()
 
 def hand_over(*refs):
@@ -493,16 +510,16 @@
         out_specs=(any_space, any_space, any_space, any_space),
         scratch_shapes=[
             pltpu.VMEM((NH, 12 * T, 2 * HD), BF),
-            pltpu.VMEM((NH, 2, T, 2 * HD), BF),
+            pltpu.VMEM((NH, T, 2 * HD), BF),
+            pltpu.VMEM((T, HALF), BF),
             pltpu.VMEM((2, T, HALF), BF),
             pltpu.VMEM((2, T, HALF), BF),
-            pltpu.VMEM((2, T, HALF), BF),
-            pltpu.VMEM((2, T, HALF), BF),
+            pltpu.VMEM((T, HALF), BF),
             pltpu.VMEM((4, T, FULL), BF),
             pltpu.VMEM((4 * FULL, HALF), BF),
             pltpu.VMEM((4 * FULL, HALF), BF),
             pltpu.VMEM((2, T, HALF), BF),
-            pltpu.VMEM((2, T, HALF), BF),
+            pltpu.VMEM((T, HALF), BF),
             pltpu.VMEM((2, T, HALF), BF),
             pltpu.VMEM((2, T, WIN), BF),
             pltpu.VMEM((2, 1, WIN), F32),
@@ -528,16 +545,16 @@
             dma((NH, 2, 3)),
             dma((NH, 2)),
             dma((NH, 2)),
-            dma((NH, 2, 2)),
-            dma((NH, 2, 2)),
+            dma((NH, 2)),
+            dma((NH, 2)),
             dma((3,)),
             dma((3,)),
-            dma((4,)),
-            dma((4,)),
-            dma((NH, 2)),
-            dma((NH, 2)),
-            dma((NH, 2)),
-            dma((NH, 2)),
+            dma((2,)),
+            dma((2,)),
+            dma((NH,)),
+            dma((NH,)),
+            dma((NH,)),
+            dma((NH,)),
             dma((2,)),
             dma((2,)),
             dma((NH, 4)),

time: 94.6 us -> 79.2 us (0.84)
  the two profiles are of different devices: /device:TPU:32 before, /device:TPU:40 now
where the time goes in v4:
time: 79.2 us; the launch traced here: 79.1 us
  Pallas kernels  78.5 us (99%)
    pallas_call x1, Pallas kernels, on_device(): pl.pallas_call(kernel, out_shape=(block, block, block, block), in_specs=[...  76.2 us
    pallas_call x1, Pallas kernels, on_device(): pl.pallas_call(hand_over, out_shape=(block, block, block, block), in_spec...  2.27 us

profile of v4, /device:TPU:40, one launch (start us, length us, event | category | flops | bytes accessed | tf_op | source)
XLA Modules:
  0.0 79.1 jit_solution(4185498708278058788)
XLA Ops:
  0.6 76.2 %shard_map.93 = (bf16[160,768]{1,0:T(8,128)(2,1)}, bf16[160,768]{1,0:T(8,128)(2,1)}, bf16[160,768]{1,0:T(8,128)(2,1)}, bf16[160,768]{1,0:T(8,128)(2,1)}) custom-call(bf16[160,768]{1,0:T(8,128)(2,1)} %q_in.1, bf16[160,768]{1,0:T(8,128)(2,1)} %k_in.1, bf16[160,768]{1,0:T(8,128)(2,1)} %v_in.1, bf16[3072,768]{1,0:T(8,128)(2,1)} %w_in.1, bf16[160,768]{1,0:T(8,128)(2,1)} %g_in.1, ...), custom_call_target="tpu_custom_call" | custom-call | tf_op jit(solution)/shard_map/pallas_call | solution.py:506
  76.9 2.3 %shard_map.94 = (bf16[160,768]{1,0:T(8,128)(2,1)}, bf16[160,768]{1,0:T(8,128)(2,1)}, bf16[160,768]{1,0:T(8,128)(2,1)}, bf16[160,768]{1,0:T(8,128)(2,1)}) custom-call(bf16[160,768]{1,0:T(8,128)(2,1)} %get-tuple-element.8.refs_0_, bf16[160,768]{1,0:T(8,128)(2,1)} %get-tuple-element.9.refs_1_, bf16[160,768]{1,0:T(8,128)(2,1)} %get-tuple-element.10.refs_2_, ...), custom_call_target="tpu_custom_call" | custom-call | tf_op jit(solution)/shard_map/pallas_call | solution.py:570

commit v5 on v4

--- a/solution.py
+++ b/solution.py
@@ -14,6 +14,7 @@
 FULL = 2 * HALF
 WIN = 9 * T
 SIDE = 3 * T
+LOG2E = 1.4426950408889634
 MESH = pl.DeviceIdType.MESH
 BF = jnp.bfloat16
 F32 = jnp.float32
@@ -34,7 +35,7 @@
 def kernel(
     q_in, k_in, v_in, w_in, g_in, valid,
     mixed, dq_out, dk_out, dv_out,
-    kv, kvo, qo, qb, dob, dop, gall, wm, wo, att, attr, dqb, pb, bias,
+    kv, kvo, qo, qb, dob, dop, gall, wm, wo, att, attr, dqb, pb, rb_sum, bias,
     xs, rx, acc, zs, rz, ys, ms, mr, ms2, mr2, mo, rb, rb2, rc,
     lsem, hsem, fs, fr, bxs, bxr, bzs, bzr, bys, byr, gs, gr, qs, qr, dqs, dqr, ats, atr, mss, msr, rls, rlr, bcs, bcr,
 ):
@@ -174,6 +175,7 @@
     ]
 
     lanes = lax.broadcasted_iota(jnp.int32, (1, WIN), 1)
+    ones = jnp.ones((WIN, HD), BF)
     for a in range(2):
         row = jnp.zeros((1, WIN), F32)
         for n in range(9):
@@ -277,24 +279,28 @@
             arrived(slot(h, s), fr.at[h, s], there)
         for a in range(2):
             window = pl.ds(a * SIDE, WIN)
-            s = nt(qb[a, :, cols(h)], kv[h, window, pl.ds(0, HD)]) * scale + bias[a]
-            x = jnp.exp(s - jnp.max(s, axis=1, keepdims=True))
-            weights = (x * (1.0 / jnp.sum(x, axis=1, keepdims=True))).astype(BF)
-            pb[a] = weights
-            att[a, :, cols(h)] = nn(weights, kv[h, window, pl.ds(HD, HD)]).astype(BF)
+            s = nt(qb[a, :, cols(h)], kv[h, window, pl.ds(0, HD)]) * (scale * LOG2E) + bias[a]
+            x = jnp.exp2(s - jnp.max(s, axis=1, keepdims=True)).astype(BF)
+            pb[a] = x
+            total = nn(x, jnp.concatenate([kv[h, window, pl.ds(HD, HD)], ones], axis=1))
+            inverse = 1.0 / total[:, HD:]
+            rb_sum[a] = inverse
+            att[a, :, cols(h)] = (total[:, :HD] * inverse).astype(BF)
         send_attended(START, h)
 
     def differentiate(h, a):
         q = qb[a, :, cols(h)]
-        do = dob[a, :, cols(h)]
+        do = dob[a, :, cols(h)].astype(F32)
         window = pl.ds(a * SIDE, WIN)
         k = kv[h, window, pl.ds(0, HD)]
         weights = pb[a]
-        row_dot = jnp.sum(do.astype(F32) * att[a, :, cols(h)].astype(F32), axis=1, keepdims=True)
-        weight_grad = nt(do, kv[h, window, pl.ds(HD, HD)])
-        score_grad = (weights.astype(F32) * (weight_grad - row_dot) * scale).astype(BF)
+        inverse = rb_sum[a]
+        row_dot = jnp.sum(do * att[a, :, cols(h)].astype(F32) * (inverse * scale), axis=1, keepdims=True)
+        do_sum = (do * inverse).astype(BF)
+        weight_grad = nt((do * (inverse * scale)).astype(BF), kv[h, window, pl.ds(HD, HD)])
+        score_grad = weights * (weight_grad - row_dot).astype(BF)
         dqb[a, :, cols(h)] = nn(score_grad, k).astype(BF)
-        for part, lhs, rhs in ((0, score_grad, q), (1, weights, do)):
+        for part, lhs, rhs in ((0, score_grad, q), (1, weights, do_sum)):
             grad = tn(lhs, rhs)
             lane = pl.ds(part * HD, HD)
             if a == 0:
@@ -378,30 +384,33 @@
     send_swap(START, 1)
     arrived(slot(0, 7), fr.at[0, 7])
     send_z(START, 0, 7)
-    for copy in kept_tiles[1]:
-        copy.wait()
-    send_z(START, 1, 4)
     g_copy.wait()
     send_gathered(START, 0)
     send_own_x(START, 0)
+    for copy in kept_tiles[1]:
+        copy.wait()
+    send_z(START, 1, 4)
+    for copy in staged[2]:
+        copy.wait()
+    send_swap(START, 2)
+    arrived(slot(1, 7), fr.at[1, 7])
+    send_z(START, 1, 7)
+    forward(START, 0, 0, 0)
+    send_other_x(START, 0)
+    forward(START, 0, 0, 1)
+    forward(START, 0, 1, 0)
+    qo_copy.wait()
+    send_queries(START)
+    send_other_x(START, 1)
+    send_own_x(START, 1)
     arrived(gall.at[2], gr.at[1])
     send_gathered(START, 2)
-    arrived(slot(1, 7), fr.at[1, 7])
-    send_z(START, 1, 7)
-    forward(START, 0, 1, 0)
-    for copy in staged[2]:
-        copy.wait()
-    send_swap(START, 2)
-    forward(START, 0, 0, 0)
     send_gathered(START, 1)
+    forward(START, 0, 1, 1)
     arrived(rb.at[0], rlr.at[0, 0], is_relay)
     pass_on(START, 0)
-    forward(START, 0, 0, 1)
-    send_other_x(START, 0)
-    qo_copy.wait()
-    send_queries(START)
-    forward(START, 0, 1, 1)
-    send_own_x(START, 1)
+    arrived(slot(2, 7), fr.at[2, 7])
+    send_z(START, 2, 7)
     forward(START, 1, 0, 0)
     for copy in w_copies:
         copy.wait()
@@ -410,50 +419,47 @@
     dop[...] = attn_grad(wo)
     send_attn_grad(START)
     dob[0] = attn_grad(wm)
-    arrived(slot(2, 7), fr.at[2, 7])
-    send_z(START, 2, 7)
     for copy in kept_tiles[2]:
         copy.wait()
     send_z(START, 2, 4)
+    forward(START, 1, 1, 1)
+    send_other_x(START, 2)
+    send_own_x(START, 2)
     arrived(rb.at[1], rlr.at[1, 0], is_relay)
     pass_on(START, 1)
-    send_other_x(START, 1)
-    send_own_x(START, 2)
     forward(START, 1, 0, 1)
-    send_other_x(START, 2)
     q_copy.wait()
     arrived(qb.at[1], qr.at[0])
     attend(0)
-    forward(START, 1, 1, 1)
     forward(START, 1, 1, 0)
     arrived(dob.at[1], qr.at[1])
     differentiate(0, 0)
     differentiate(0, 1)
+    forward(START, 2, 1, 1)
+    forward(START, 2, 1, 0)
     forward(START, 2, 0, 0)
+    attend(1)
+    forward(START, 2, 0, 1)
     arrived(rb2.at[0], rlr.at[0, 1], is_relay)
     pass_back(START, 0)
-    forward(START, 2, 1, 0)
-    attend(1)
     arrived(rb.at[2], rlr.at[2, 0], is_relay)
     pass_on(START, 2)
-    forward(START, 2, 0, 1)
-    forward(START, 2, 1, 1)
     differentiate(1, 0)
     differentiate(1, 1)
     reduce_x(0)
+    attend(2)
     arrived(rb2.at[1], rlr.at[1, 1], is_relay)
     pass_back(START, 1)
-    attend(2)
     differentiate(2, 0)
     differentiate(2, 1)
     reduce_x(1)
-    arrived(rb2.at[2], rlr.at[2, 1], is_relay)
-    pass_back(START, 2)
     for h in range(NH):
         arrived(attr.at[:, cols(h)], atr.at[h])
     ms[0] = project(3).astype(BF)
     ms[1] = project(1).astype(BF)
     remote(START, ms, mr, mss.at[0], msr.at[0], sibling)
+    arrived(rb2.at[2], rlr.at[2, 1], is_relay)
+    pass_back(START, 2)
     crossing_sum = project(2)
     arrived(mr, msr.at[0])
     ms2[...] = (crossing_sum + mr[0].astype(F32)).astype(BF)
@@ -522,6 +528,7 @@
             pltpu.VMEM((T, HALF), BF),
             pltpu.VMEM((2, T, HALF), BF),
             pltpu.VMEM((2, T, WIN), BF),
+            pltpu.VMEM((2, T, HD), F32),
             pltpu.VMEM((2, 1, WIN), F32),
             pltpu.VMEM((NH, 2, SIDE, 2 * HD), BF),
             pltpu.VMEM((NH, 2, SIDE, 2 * HD), BF),

time: 79.2 us -> 79 us (level)
  the two profiles are of different devices: /device:TPU:40 before, /device:TPU:32 now
where the time goes in v5:
time: 79 us; the launch traced here: 78.9 us
  Pallas kernels  78.3 us (99%)
    pallas_call x1, Pallas kernels, on_device(): pl.pallas_call(kernel, out_shape=(block, block, block, block), in_specs=[...  76 us
    pallas_call x1, Pallas kernels, on_device(): pl.pallas_call(hand_over, out_shape=(block, block, block, block), in_spec...  2.27 us

profile of v5, /device:TPU:32, one launch (start us, length us, event | category | flops | bytes accessed | tf_op | source)
XLA Modules:
  0.0 78.9 jit_solution(15596508205115220869)
XLA Ops:
  0.6 76.0 %shard_map.93 = (bf16[160,768]{1,0:T(8,128)(2,1)}, bf16[160,768]{1,0:T(8,128)(2,1)}, bf16[160,768]{1,0:T(8,128)(2,1)}, bf16[160,768]{1,0:T(8,128)(2,1)}) custom-call(bf16[160,768]{1,0:T(8,128)(2,1)} %q_in.1, bf16[160,768]{1,0:T(8,128)(2,1)} %k_in.1, bf16[160,768]{1,0:T(8,128)(2,1)} %v_in.1, bf16[3072,768]{1,0:T(8,128)(2,1)} %w_in.1, bf16[160,768]{1,0:T(8,128)(2,1)} %g_in.1, ...), custom_call_target="tpu_custom_call" | custom-call | tf_op jit(solution)/shard_map/pallas_call | solution.py:512
  76.6 2.3 %shard_map.94 = (bf16[160,768]{1,0:T(8,128)(2,1)}, bf16[160,768]{1,0:T(8,128)(2,1)}, bf16[160,768]{1,0:T(8,128)(2,1)}, bf16[160,768]{1,0:T(8,128)(2,1)}) custom-call(bf16[160,768]{1,0:T(8,128)(2,1)} %get-tuple-element.8.refs_0_, bf16[160,768]{1,0:T(8,128)(2,1)} %get-tuple-element.9.refs_1_, bf16[160,768]{1,0:T(8,128)(2,1)} %get-tuple-element.10.refs_2_, ...), custom_call_target="tpu_custom_call" | custom-call | tf_op jit(solution)/shard_map/pallas_call | solution.py:577

commit v6 on v5

--- a/solution.py
+++ b/solution.py
@@ -15,6 +15,8 @@
 WIN = 9 * T
 SIDE = 3 * T
 LOG2E = 1.4426950408889634
+DIRECT_OUT = (0,)
+DIRECT_BACK = (2,)
 MESH = pl.DeviceIdType.MESH
 BF = jnp.bfloat16
 F32 = jnp.float32
@@ -195,8 +197,10 @@
 
     def send_side(act, h, s, target, n, device, there, crossing):
         tile = slot(h, s)
-        remote(act, tile, slot(h, target), fs.at[h, n], fr.at[h, target], device, there & jnp.logical_not(crossing))
-        remote(act, tile, rb.at[h], rls.at[h, 0], rlr.at[h, 0], relay, crossing)
+        direct = there if h in DIRECT_OUT else there & jnp.logical_not(crossing)
+        remote(act, tile, slot(h, target), fs.at[h, n], fr.at[h, target], device, direct)
+        if h not in DIRECT_OUT:
+            remote(act, tile, rb.at[h], rls.at[h, 0], rlr.at[h, 0], relay, crossing)
         remote(
             act, tile, slot(h, target + e), fs.at[h, n + 1], fr.at[h, target + e], back, crossing & has_back
         )
@@ -215,6 +219,10 @@
         send_side(act, h, 7, 1, 6, far, has_far, far_cross)
 
     def pass_on(act, h):
+        if h in DIRECT_OUT:
+            return
+        if act == START:
+            arrived(rb.at[h], rlr.at[h, 0], is_relay)
         target = jnp.where((u == 0) == (p == 1), 10, 1)
         remote(act, rb.at[h], slot(h, target), rls.at[h, 1], fr.at[h, target], relay_to, is_relay)
 
@@ -235,7 +243,11 @@
             act, xs.at[h, n], rx.at[h, n], bxs.at[h, n, 0], bxr.at[h, n, 0], device,
             there & jnp.logical_not(crossing),
         )
-        remote(act, xs.at[h, n, pl.ds(T, T)], rb2.at[h], rls.at[h, 2], rlr.at[h, 1], relay, crossing)
+        middle = xs.at[h, n, pl.ds(T, T)]
+        if h in DIRECT_BACK:
+            remote(act, middle, rx.at[h, n, pl.ds(T, T)], bxs.at[h, n, 2], bxr.at[h, n, 1], device, crossing)
+        else:
+            remote(act, middle, rb2.at[h], rls.at[h, 2], rlr.at[h, 1], relay, crossing)
         rows = pl.ds((1 + e) * T, T)
         remote(
             act, xs.at[h, n, rows], rx.at[h, n, rows], bxs.at[h, n, 1], bxr.at[h, n, 2], device, crossing & has_ahead
@@ -245,6 +257,10 @@
         )
 
     def pass_back(act, h):
+        if h in DIRECT_BACK:
+            return
+        if act == START:
+            arrived(rb2.at[h], rlr.at[h, 1], is_relay)
         n = jnp.where(u == 0, p, 1 - p)
         remote(act, rb2.at[h], rx.at[h, n, pl.ds(T, T)], rls.at[h, 3], bxr.at[h, n, 1], relay_to, is_relay)
 
@@ -407,7 +423,6 @@
     send_gathered(START, 2)
     send_gathered(START, 1)
     forward(START, 0, 1, 1)
-    arrived(rb.at[0], rlr.at[0, 0], is_relay)
     pass_on(START, 0)
     arrived(slot(2, 7), fr.at[2, 7])
     send_z(START, 2, 7)
@@ -425,7 +440,6 @@
     forward(START, 1, 1, 1)
     send_other_x(START, 2)
     send_own_x(START, 2)
-    arrived(rb.at[1], rlr.at[1, 0], is_relay)
     pass_on(START, 1)
     forward(START, 1, 0, 1)
     q_copy.wait()
@@ -440,15 +454,12 @@
     forward(START, 2, 0, 0)
     attend(1)
     forward(START, 2, 0, 1)
-    arrived(rb2.at[0], rlr.at[0, 1], is_relay)
     pass_back(START, 0)
-    arrived(rb.at[2], rlr.at[2, 0], is_relay)
     pass_on(START, 2)
     differentiate(1, 0)
     differentiate(1, 1)
     reduce_x(0)
     attend(2)
-    arrived(rb2.at[1], rlr.at[1, 1], is_relay)
     pass_back(START, 1)
     differentiate(2, 0)
     differentiate(2, 1)
@@ -458,7 +469,6 @@
     ms[0] = project(3).astype(BF)
     ms[1] = project(1).astype(BF)
     remote(START, ms, mr, mss.at[0], msr.at[0], sibling)
-    arrived(rb2.at[2], rlr.at[2, 1], is_relay)
     pass_back(START, 2)
     crossing_sum = project(2)
     arrived(mr, msr.at[0])
@@ -501,8 +511,16 @@
     mixed_copy.wait()
 
 def hand_over(*refs):
+    sources, results, held, ins, outs = refs[:4], refs[4:8], refs[8], refs[9], refs[10]
+    arriving = [pltpu.make_async_copy(sources[n], held.at[n], ins.at[n]) for n in range(4)]
+    leaving = [pltpu.make_async_copy(held.at[n], results[n], outs.at[n]) for n in range(4)]
+    for copy in arriving:
+        copy.start()
     for n in range(4):
-        refs[4 + n][...] = refs[n][...]
+        arriving[n].wait()
+        leaving[n].start()
+    for copy in leaving:
+        copy.wait()
 
 
 def on_device(queries, keys, values, w_out, out_grad, tile_valid):
@@ -548,7 +566,7 @@
             dma((NH, 4)),
             dma((NH, 14)),
             dma((NH, 12)),
-            dma((NH, 2, 2)),
+            dma((NH, 2, 3)),
             dma((NH, 2, 3)),
             dma((NH, 2)),
             dma((NH, 2)),
@@ -573,12 +591,13 @@
             collective_id=0, has_side_effects=True, vmem_limit_bytes=56 * 1024 * 1024
         ),
     )(queries, keys, values, w_out, out_grad, tile_valid)
-    whole = pl.BlockSpec(memory_space=pltpu.VMEM)
     return pl.pallas_call(
         hand_over,
         out_shape=(block, block, block, block),
-        in_specs=[whole] * 4,
-        out_specs=(whole, whole, whole, whole),
+        in_specs=[any_space] * 4,
+        out_specs=(any_space, any_space, any_space, any_space),
+        scratch_shapes=[pltpu.VMEM((4, *queries.shape), BF), dma((4,)), dma((4,))],
+        compiler_params=pltpu.CompilerParams(vmem_limit_bytes=56 * 1024 * 1024),
     )(*results)
 
 

time: 79 us -> 78.1 us (0.989)
  Pallas kernels: 78.3 us -> 77 us
    pallas_call x1, Pallas kernels: 76 us -> 74.9 us  [on_device(): pl.pallas_call(kernel, out_shape=(block, block, block, block), in_specs=[...]
where the time goes in v6:
time: 78.1 us; the launch traced here: 77.6 us
  Pallas kernels  77 us (99%)
    pallas_call x1, Pallas kernels, on_device(): pl.pallas_call(kernel, out_shape=(block, block, block, block), in_specs=[...  74.9 us
    pallas_call x1, Pallas kernels, on_device(): pl.pallas_call(hand_over, out_shape=(block, block, block, block), in_spec...  2.07 us

profile of v6, /device:TPU:32, one launch (start us, length us, event | category | flops | bytes accessed | tf_op | source)
XLA Modules:
  0.0 77.6 jit_solution(8574900484465947715)
XLA Ops:
  0.6 74.9 %shard_map.93 = (bf16[160,768]{1,0:T(8,128)(2,1)}, bf16[160,768]{1,0:T(8,128)(2,1)}, bf16[160,768]{1,0:T(8,128)(2,1)}, bf16[160,768]{1,0:T(8,128)(2,1)}) custom-call(bf16[160,768]{1,0:T(8,128)(2,1)} %q_in.1, bf16[160,768]{1,0:T(8,128)(2,1)} %k_in.1, bf16[160,768]{1,0:T(8,128)(2,1)} %v_in.1, bf16[3072,768]{1,0:T(8,128)(2,1)} %w_in.1, bf16[160,768]{1,0:T(8,128)(2,1)} %g_in.1, ...), custom_call_target="tpu_custom_call" | custom-call | tf_op jit(solution)/shard_map/pallas_call | solution.py:530
  75.6 2.1 %shard_map.94 = (bf16[160,768]{1,0:T(8,128)(2,1)}, bf16[160,768]{1,0:T(8,128)(2,1)}, bf16[160,768]{1,0:T(8,128)(2,1)}, bf16[160,768]{1,0:T(8,128)(2,1)}) custom-call(bf16[160,768]{1,0:T(8,128)(2,1)} %get-tuple-element.8.refs_0_, bf16[160,768]{1,0:T(8,128)(2,1)} %get-tuple-element.9.refs_1_, bf16[160,768]{1,0:T(8,128)(2,1)} %get-tuple-element.10.refs_2_, ...), custom_call_target="tpu_custom_call" | custom-call | tf_op jit(solution)/shard_map/pallas_call | solution.py:594

commit v7 on v6

--- a/solution.py
+++ b/solution.py
@@ -17,6 +17,7 @@
 LOG2E = 1.4426950408889634
 DIRECT_OUT = (0,)
 DIRECT_BACK = (2,)
+SPLIT = (2,)
 MESH = pl.DeviceIdType.MESH
 BF = jnp.bfloat16
 F32 = jnp.float32
@@ -237,23 +238,35 @@
             exists & there & (jnp.logical_not(crossing) | (e == way)),
         )
 
-    def send_back(act, h, n):
+    def parts_of(h):
+        return (1, 0) if h in SPLIT else (None,)
+
+    def lanes_of(part):
+        return (0, pl.ds(0, 2 * HD)) if part is None else (part, pl.ds(part * HD, HD))
+
+    def send_back(act, h, n, part):
+        k, lane = lanes_of(part)
         device, there, crossing = ((far, has_far, far_cross), (near, has_near, near_cross))[n]
         remote(
-            act, xs.at[h, n], rx.at[h, n], bxs.at[h, n, 0], bxr.at[h, n, 0], device,
+            act, xs.at[h, n, :, lane], rx.at[h, n, :, lane], bxs.at[h, n, k, 0], bxr.at[h, n, k, 0], device,
             there & jnp.logical_not(crossing),
         )
-        middle = xs.at[h, n, pl.ds(T, T)]
+        middle = pl.ds(T, T)
         if h in DIRECT_BACK:
-            remote(act, middle, rx.at[h, n, pl.ds(T, T)], bxs.at[h, n, 2], bxr.at[h, n, 1], device, crossing)
+            remote(
+                act, xs.at[h, n, middle, lane], rx.at[h, n, middle, lane], bxs.at[h, n, k, 2], bxr.at[h, n, k, 1],
+                device, crossing,
+            )
         else:
-            remote(act, middle, rb2.at[h], rls.at[h, 2], rlr.at[h, 1], relay, crossing)
+            remote(act, xs.at[h, n, middle], rb2.at[h], rls.at[h, 2], rlr.at[h, 1], relay, crossing)
         rows = pl.ds((1 + e) * T, T)
         remote(
-            act, xs.at[h, n, rows], rx.at[h, n, rows], bxs.at[h, n, 1], bxr.at[h, n, 2], device, crossing & has_ahead
+            act, xs.at[h, n, rows, lane], rx.at[h, n, rows, lane], bxs.at[h, n, k, 1], bxr.at[h, n, k, 2], device,
+            crossing & has_ahead,
         )
         remote(
-            act, xs.at[h, n, pl.ds((1 - e) * T, T)], rc.at[h], bcs.at[h, n], bcr.at[h], back, crossing & has_back
+            act, xs.at[h, n, pl.ds((1 - e) * T, T), lane], rc.at[h, :, lane], bcs.at[h, n, k], bcr.at[h, k], back,
+            crossing & has_back,
         )
 
     def pass_back(act, h):
@@ -262,7 +275,7 @@
         if act == START:
             arrived(rb2.at[h], rlr.at[h, 1], is_relay)
         n = jnp.where(u == 0, p, 1 - p)
-        remote(act, rb2.at[h], rx.at[h, n, pl.ds(T, T)], rls.at[h, 3], bxr.at[h, n, 1], relay_to, is_relay)
+        remote(act, rb2.at[h], rx.at[h, n, pl.ds(T, T)], rls.at[h, 3], bxr.at[h, n, 0, 1], relay_to, is_relay)
 
     def send_attended(act, h):
         remote(act, att.at[1, :, cols(h)], attr.at[:, cols(h)], ats.at[h], atr.at[h], partner)
@@ -275,15 +288,18 @@
         else:
             copy.wait()
 
-    def send_reduced(act, h):
-        remote(act, zs.at[h, 0], rz.at[h, 0], bzs.at[h, 0], bzr.at[h, 0], down, has_down)
-        remote(act, zs.at[h, 1], rz.at[h, 1], bzs.at[h, 1], bzr.at[h, 1], up, has_up)
-
-    def send_total(act, h):
-        for part, out in enumerate((dk_out, dv_out)):
-            lane = pl.ds(part * HD, HD)
-            remote(act, ys.at[h, 1, :, lane], out.at[:, mine_cols(h)], bys.at[h, part], byr.at[h, part], partner)
-            copy = pltpu.make_async_copy(ys.at[h, 0, :, lane], out.at[:, mine_cols(h)], hsem.at[h, part])
+    def send_reduced(act, h, part):
+        k, lane = lanes_of(part)
+        remote(act, zs.at[h, 0, :, lane], rz.at[h, 0, :, lane], bzs.at[h, 0, k], bzr.at[h, 0, k], down, has_down)
+        remote(act, zs.at[h, 1, :, lane], rz.at[h, 1, :, lane], bzs.at[h, 1, k], bzr.at[h, 1, k], up, has_up)
+
+    def send_total(act, h, part):
+        for n, out in enumerate((dk_out, dv_out)):
+            if part is not None and n != part:
+                continue
+            lane = pl.ds(n * HD, HD)
+            remote(act, ys.at[h, 1, :, lane], out.at[:, mine_cols(h)], bys.at[h, n], byr.at[h, n], partner)
+            copy = pltpu.make_async_copy(ys.at[h, 0, :, lane], out.at[:, mine_cols(h)], hsem.at[h, n])
             if act == START:
                 copy.start()
             else:
@@ -304,68 +320,80 @@
             att[a, :, cols(h)] = (total[:, :HD] * inverse).astype(BF)
         send_attended(START, h)
 
-    def differentiate(h, a):
+    def add_part(h, a, part, grad):
+        lane = pl.ds(part * HD, HD)
+        if a == 0:
+            xs[h, 1, :, lane] = grad[:SIDE].astype(BF)
+            acc[h, :, lane] = grad[SIDE:]
+        else:
+            acc[h, :, lane] += grad[:2 * SIDE]
+            xs[h, 0, :, lane] = grad[2 * SIDE:].astype(BF)
+
+    def value_part(h, a):
+        add_part(h, a, 1, tn(pb[a], (dob[a, :, cols(h)].astype(F32) * rb_sum[a]).astype(BF)))
+
+    def key_part(h, a):
         q = qb[a, :, cols(h)]
         do = dob[a, :, cols(h)].astype(F32)
         window = pl.ds(a * SIDE, WIN)
         k = kv[h, window, pl.ds(0, HD)]
-        weights = pb[a]
-        inverse = rb_sum[a]
-        row_dot = jnp.sum(do * att[a, :, cols(h)].astype(F32) * (inverse * scale), axis=1, keepdims=True)
-        do_sum = (do * inverse).astype(BF)
-        weight_grad = nt((do * (inverse * scale)).astype(BF), kv[h, window, pl.ds(HD, HD)])
-        score_grad = weights * (weight_grad - row_dot).astype(BF)
+        scaled = rb_sum[a] * scale
+        row_dot = jnp.sum(do * att[a, :, cols(h)].astype(F32) * scaled, axis=1, keepdims=True)
+        weight_grad = nt((do * scaled).astype(BF), kv[h, window, pl.ds(HD, HD)])
+        score_grad = pb[a] * (weight_grad - row_dot).astype(BF)
         dqb[a, :, cols(h)] = nn(score_grad, k).astype(BF)
-        for part, lhs, rhs in ((0, score_grad, q), (1, weights, do_sum)):
-            grad = tn(lhs, rhs)
-            lane = pl.ds(part * HD, HD)
-            if a == 0:
-                xs[h, 1, :, lane] = grad[:SIDE].astype(BF)
-                acc[h, :, lane] = grad[SIDE:]
-            else:
-                acc[h, :, lane] += grad[:2 * SIDE]
-                xs[h, 0, :, lane] = grad[2 * SIDE:].astype(BF)
-        send_back(START, h, 1 - a)
+        add_part(h, a, 0, tn(score_grad, q))
+
+    def differentiate(h, a):
+        key_part(h, a)
+        value_part(h, a)
+        send_back(START, h, 1 - a, None)
         if a == 1:
             send_query_grad(START, h)
 
-    def reduce_x(h):
+    def differentiate_values(h):
+        for a in range(2):
+            value_part(h, a)
+            send_back(START, h, 1 - a, 1)
+
+    def differentiate_keys(h):
+        for a in range(2):
+            key_part(h, a)
+            send_back(START, h, 1 - a, 0)
+        send_query_grad(START, h)
+
+    def reduce_x(h, part):
+        k, lane = lanes_of(part)
         for n, there, crossing in ((0, has_near, near_cross), (1, has_far, far_cross)):
-            arrived(rx.at[h, n], bxr.at[h, n, 0], there & jnp.logical_not(crossing))
-            arrived(rx.at[h, n, pl.ds(T, T)], bxr.at[h, n, 1], crossing)
-            arrived(rx.at[h, n, pl.ds((1 - e) * T, T)], bxr.at[h, n, 2], crossing & has_back)
+            arrived(rx.at[h, n, :, lane], bxr.at[h, n, k, 0], there & jnp.logical_not(crossing))
+            arrived(rx.at[h, n, pl.ds(T, T), lane], bxr.at[h, n, k, 1], crossing)
+            arrived(rx.at[h, n, pl.ds((1 - e) * T, T), lane], bxr.at[h, n, k, 2], crossing & has_back)
         for n in range(2):
-            for part, row in ((0, 0), (1, 2 * T)):
-                zs[h, part, pl.ds(n * T, T), :] = (
-                    acc[h, pl.ds(n * SIDE + row, T), :] + rx[h, n, pl.ds(row, T), :].astype(F32)
+            for side, row in ((0, 0), (1, 2 * T)):
+                zs[h, side, pl.ds(n * T, T), lane] = (
+                    acc[h, pl.ds(n * SIDE + row, T), lane] + rx[h, n, pl.ds(row, T), lane].astype(F32)
                 ).astype(BF)
-            acc[h, pl.ds(n * SIDE + T, T), :] += rx[h, n, pl.ds(T, T), :].astype(F32)
-        send_reduced(START, h)
-
-    def reduce_z(h):
-        arrived(rz.at[h, 0], bzr.at[h, 0], has_up)
-        arrived(rz.at[h, 1], bzr.at[h, 1], has_down)
-        arrived(rc.at[h], bcr.at[h], is_cross & has_back)
+            acc[h, pl.ds(n * SIDE + T, T), lane] += rx[h, n, pl.ds(T, T), lane].astype(F32)
+        send_reduced(START, h, part)
+
+    def reduce_z(h, part):
+        k, lane = lanes_of(part)
+        arrived(rz.at[h, 0, :, lane], bzr.at[h, 0, k], has_up)
+        arrived(rz.at[h, 1, :, lane], bzr.at[h, 1, k], has_down)
+        arrived(rc.at[h, :, lane], bcr.at[h, k], is_cross & has_back)
         for n, crossing in ((0, near_cross), (1, far_cross)):
             @pl.when(crossing & has_back)
             def _():
-                acc[h, pl.ds(n * SIDE + T, T), :] += rc[h].astype(F32)
+                acc[h, pl.ds(n * SIDE + T, T), lane] += rc[h, :, lane].astype(F32)
 
         for n in range(2):
             rows = pl.ds(n * T, T)
-            ys[h, n] = (
-                acc[h, pl.ds(n * SIDE + T, T), :] + rz[h, 0, rows, :].astype(F32) + rz[h, 1, rows, :].astype(F32)
+            ys[h, n, :, lane] = (
+                acc[h, pl.ds(n * SIDE + T, T), lane]
+                + rz[h, 0, rows, lane].astype(F32)
+                + rz[h, 1, rows, lane].astype(F32)
             ).astype(BF)
-        send_total(START, h)
-
-    blocks = (j, j1, j2, j3)
-    rows = [pl.ds(pl.multiple_of(block * FULL, FULL), FULL) for block in blocks]
-
-    def attn_grad(weights_ref):
-        total = nn(gall[0], weights_ref[rows[0], :])
-        for n in range(1, 4):
-            total = total + nn(gall[n], weights_ref[rows[n], :])
-        return total.astype(BF)
+        send_total(START, h, part)
 
     blocks = (j, j1, j2, j3)
     rows = [pl.ds(pl.multiple_of(block * FULL, FULL), FULL) for block in blocks]
@@ -458,27 +486,28 @@
     pass_on(START, 2)
     differentiate(1, 0)
     differentiate(1, 1)
-    reduce_x(0)
+    reduce_x(0, None)
     attend(2)
     pass_back(START, 1)
-    differentiate(2, 0)
-    differentiate(2, 1)
-    reduce_x(1)
+    differentiate_values(2)
+    differentiate_keys(2)
+    reduce_x(1, None)
     for h in range(NH):
         arrived(attr.at[:, cols(h)], atr.at[h])
     ms[0] = project(3).astype(BF)
     ms[1] = project(1).astype(BF)
     remote(START, ms, mr, mss.at[0], msr.at[0], sibling)
-    pass_back(START, 2)
+    reduce_x(2, 1)
     crossing_sum = project(2)
     arrived(mr, msr.at[0])
     ms2[...] = (crossing_sum + mr[0].astype(F32)).astype(BF)
     remote(START, ms2, mr2, mss.at[1], msr.at[1], across)
     kept = project(0) + mr[1].astype(F32)
-    reduce_x(2)
-    reduce_z(0)
-    reduce_z(1)
-    reduce_z(2)
+    reduce_x(2, 0)
+    reduce_z(0, None)
+    reduce_z(1, None)
+    reduce_z(2, 1)
+    reduce_z(2, 0)
     arrived(mr2, msr.at[1])
     mo[...] = (kept + mr2[...].astype(F32)).astype(BF)
     mixed_copy = local(mo, mixed, lsem.at[5])
@@ -497,14 +526,17 @@
     remote(WAIT, ms2, mr2, mss.at[1], msr.at[1], across)
     for h in range(NH):
         for send in (
-            send_swap, send_own_x, send_other_x, pass_on, pass_back, send_attended, send_query_grad, send_reduced,
-            send_total,
+            send_swap, send_own_x, send_other_x, pass_on, pass_back, send_attended, send_query_grad,
         ):
             send(WAIT, h)
         for n in range(2):
             forward(WAIT, h, n, 0)
             forward(WAIT, h, n, 1)
-            send_back(WAIT, h, n)
+            for part in parts_of(h):
+                send_back(WAIT, h, n, part)
+        for part in parts_of(h):
+            send_reduced(WAIT, h, part)
+            send_total(WAIT, h, part)
         arrived(dq_out.at[:, their_cols(h)], dqr.at[h])
         arrived(dk_out.at[:, their_cols(h)], byr.at[h, 0])
         arrived(dv_out.at[:, their_cols(h)], byr.at[h, 1])
@@ -566,10 +598,10 @@
             dma((NH, 4)),
             dma((NH, 14)),
             dma((NH, 12)),
-            dma((NH, 2, 3)),
-            dma((NH, 2, 3)),
-            dma((NH, 2)),
-            dma((NH, 2)),
+            dma((NH, 2, 2, 3)),
+            dma((NH, 2, 2, 3)),
+            dma((NH, 2, 2)),
+            dma((NH, 2, 2)),
             dma((NH, 2)),
             dma((NH, 2)),
             dma((3,)),
@@ -584,8 +616,8 @@
             dma((2,)),
             dma((NH, 4)),
             dma((NH, 2)),
+            dma((NH, 2, 2)),
             dma((NH, 2)),
-            dma((NH,)),
         ],
         compiler_params=pltpu.CompilerParams(
             collective_id=0, has_side_effects=True, vmem_limit_bytes=56 * 1024 * 1024

time: 78.1 us -> 78 us (level)
  no operation moved by 1% of the time
where the time goes in v7:
time: 78 us; the launch traced here: 77.7 us
  Pallas kernels  77.1 us (99%)
    pallas_call x1, Pallas kernels, on_device(): pl.pallas_call(kernel, out_shape=(block, block, block, block), in_specs=[...  75 us
    pallas_call x1, Pallas kernels, on_device(): pl.pallas_call(hand_over, out_shape=(block, block, block, block), in_spec...  2.07 us

profile of v7, /device:TPU:32, one launch (start us, length us, event | category | flops | bytes accessed | tf_op | source)
XLA Modules:
  0.0 77.7 jit_solution(15816602168590536297)
XLA Ops:
  0.6 75.0 %shard_map.93 = (bf16[160,768]{1,0:T(8,128)(2,1)}, bf16[160,768]{1,0:T(8,128)(2,1)}, bf16[160,768]{1,0:T(8,128)(2,1)}, bf16[160,768]{1,0:T(8,128)(2,1)}) custom-call(bf16[160,768]{1,0:T(8,128)(2,1)} %q_in.1, bf16[160,768]{1,0:T(8,128)(2,1)} %k_in.1, bf16[160,768]{1,0:T(8,128)(2,1)} %v_in.1, bf16[3072,768]{1,0:T(8,128)(2,1)} %w_in.1, bf16[160,768]{1,0:T(8,128)(2,1)} %g_in.1, ...), custom_call_target="tpu_custom_call" | custom-call | tf_op jit(solution)/shard_map/pallas_call | solution.py:562
  75.6 2.1 %shard_map.94 = (bf16[160,768]{1,0:T(8,128)(2,1)}, bf16[160,768]{1,0:T(8,128)(2,1)}, bf16[160,768]{1,0:T(8,128)(2,1)}, bf16[160,768]{1,0:T(8,128)(2,1)}) custom-call(bf16[160,768]{1,0:T(8,128)(2,1)} %get-tuple-element.8.refs_0_, bf16[160,768]{1,0:T(8,128)(2,1)} %get-tuple-element.9.refs_1_, bf16[160,768]{1,0:T(8,128)(2,1)} %get-tuple-element.10.refs_2_, ...), custom_call_target="tpu_custom_call" | custom-call | tf_op jit(solution)/shard_map/pallas_call | solution.py:626

commit v8 on v7

--- a/solution.py
+++ b/solution.py
@@ -17,7 +17,7 @@
 LOG2E = 1.4426950408889634
 DIRECT_OUT = (0,)
 DIRECT_BACK = (2,)
-SPLIT = (2,)
+SPLIT = ()
 MESH = pl.DeviceIdType.MESH
 BF = jnp.bfloat16
 F32 = jnp.float32
@@ -38,8 +38,8 @@
 def kernel(
     q_in, k_in, v_in, w_in, g_in, valid,
     mixed, dq_out, dk_out, dv_out,
-    kv, kvo, qo, qb, dob, dop, gall, wm, wo, att, attr, dqb, pb, rb_sum, bias,
-    xs, rx, acc, zs, rz, ys, ms, mr, ms2, mr2, mo, rb, rb2, rc,
+    kv, kvo, qo, qb, dob, dop, gall, wm, wo, att, attr, dqb, dql, pb, rb_sum, bias,
+    xs, rx, acc, zs, rz, ys, yr, ms, mr, ms2, mr2, res, kin, vin, qin, rb, rb2, rc,
     lsem, hsem, fs, fr, bxs, bxr, bzs, bzr, bys, byr, gs, gr, qs, qr, dqs, dqr, ats, atr, mss, msr, rls, rlr, bcs, bcr,
 ):
     i = lax.axis_index("tile")
@@ -155,23 +155,10 @@
         copy.start()
         return copy
 
-    staged = [
-        [
-            local(k_in.at[:, their_cols(h)], kvo.at[h, :, pl.ds(0, HD)], hsem.at[h, 0]),
-            local(v_in.at[:, their_cols(h)], kvo.at[h, :, pl.ds(HD, HD)], hsem.at[h, 1]),
-        ]
-        for h in range(NH)
-    ]
-    kept_tiles = [
-        [
-            local(k_in.at[:, mine_cols(h)], slot(h, 4).at[:, pl.ds(0, HD)], hsem.at[h, 2]),
-            local(v_in.at[:, mine_cols(h)], slot(h, 4).at[:, pl.ds(HD, HD)], hsem.at[h, 3]),
-        ]
-        for h in range(NH)
-    ]
+    k_copy = local(k_in, kin, hsem.at[0])
+    v_copy = local(v_in, vin, hsem.at[1])
     g_copy = local(g_in, gall.at[0], lsem.at[0])
-    q_copy = local(q_in.at[:, pl.ds(mine, HALF)], qb.at[0], lsem.at[1])
-    qo_copy = local(q_in.at[:, pl.ds(theirs, HALF)], qo, lsem.at[2])
+    q_copy = local(q_in, qin, lsem.at[1])
     w_copies = [
         local(w_in.at[:, pl.ds(theirs, HALF)], wo, lsem.at[3]),
         local(w_in.at[:, pl.ds(mine, HALF)], wm, lsem.at[4]),
@@ -281,29 +268,15 @@
         remote(act, att.at[1, :, cols(h)], attr.at[:, cols(h)], ats.at[h], atr.at[h], partner)
 
     def send_query_grad(act, h):
-        remote(act, dqb.at[1, :, cols(h)], dq_out.at[:, mine_cols(h)], dqs.at[h], dqr.at[h], partner)
-        copy = pltpu.make_async_copy(dqb.at[0, :, cols(h)], dq_out.at[:, mine_cols(h)], hsem.at[h, 2])
-        if act == START:
-            copy.start()
-        else:
-            copy.wait()
+        remote(act, dqb.at[:, cols(h)], dql.at[:, cols(h)], dqs.at[h], dqr.at[h], partner)
 
     def send_reduced(act, h, part):
         k, lane = lanes_of(part)
         remote(act, zs.at[h, 0, :, lane], rz.at[h, 0, :, lane], bzs.at[h, 0, k], bzr.at[h, 0, k], down, has_down)
         remote(act, zs.at[h, 1, :, lane], rz.at[h, 1, :, lane], bzs.at[h, 1, k], bzr.at[h, 1, k], up, has_up)
 
-    def send_total(act, h, part):
-        for n, out in enumerate((dk_out, dv_out)):
-            if part is not None and n != part:
-                continue
-            lane = pl.ds(n * HD, HD)
-            remote(act, ys.at[h, 1, :, lane], out.at[:, mine_cols(h)], bys.at[h, n], byr.at[h, n], partner)
-            copy = pltpu.make_async_copy(ys.at[h, 0, :, lane], out.at[:, mine_cols(h)], hsem.at[h, n])
-            if act == START:
-                copy.start()
-            else:
-                copy.wait()
+    def send_total(act, h):
+        remote(act, ys.at[h], yr.at[h], bys.at[h], byr.at[h], partner)
 
     def attend(h):
         for s, there in ((9, has_far & has_down), (10, has_far), (11, has_far & has_up),
@@ -341,7 +314,11 @@
         row_dot = jnp.sum(do * att[a, :, cols(h)].astype(F32) * scaled, axis=1, keepdims=True)
         weight_grad = nt((do * scaled).astype(BF), kv[h, window, pl.ds(HD, HD)])
         score_grad = pb[a] * (weight_grad - row_dot).astype(BF)
-        dqb[a, :, cols(h)] = nn(score_grad, k).astype(BF)
+        query_grad = nn(score_grad, k).astype(BF)
+        if a == 0:
+            res[1, :, mine_cols(h)] = query_grad
+        else:
+            dqb[:, cols(h)] = query_grad
         add_part(h, a, 0, tn(score_grad, q))
 
     def differentiate(h, a):
@@ -350,17 +327,6 @@
         send_back(START, h, 1 - a, None)
         if a == 1:
             send_query_grad(START, h)
-
-    def differentiate_values(h):
-        for a in range(2):
-            value_part(h, a)
-            send_back(START, h, 1 - a, 1)
-
-    def differentiate_keys(h):
-        for a in range(2):
-            key_part(h, a)
-            send_back(START, h, 1 - a, 0)
-        send_query_grad(START, h)
 
     def reduce_x(h, part):
         k, lane = lanes_of(part)
@@ -386,15 +352,21 @@
             def _():
                 acc[h, pl.ds(n * SIDE + T, T), lane] += rc[h, :, lane].astype(F32)
 
-        for n in range(2):
-            rows = pl.ds(n * T, T)
-            ys[h, n, :, lane] = (
-                acc[h, pl.ds(n * SIDE + T, T), lane]
-                + rz[h, 0, rows, lane].astype(F32)
-                + rz[h, 1, rows, lane].astype(F32)
+        sums = [
+            (
+                acc[h, pl.ds(n * SIDE + T, T), :]
+                + rz[h, 0, pl.ds(n * T, T), :].astype(F32)
+                + rz[h, 1, pl.ds(n * T, T), :].astype(F32)
             ).astype(BF)
-        send_total(START, h, part)
-
+            for n in range(2)
+        ]
+        ys[h] = sums[1]
+        send_total(START, h)
+        res[2, :, mine_cols(h)] = sums[0][:, :HD]
+        res[3, :, mine_cols(h)] = sums[0][:, HD:]
+
+    k_copy.wait()
+    v_copy.wait()
     blocks = (j, j1, j2, j3)
     rows = [pl.ds(pl.multiple_of(block * FULL, FULL), FULL) for block in blocks]
 
@@ -417,25 +389,25 @@
     def project(n):
         return nt(att[0], wm[rows[n], :]) + nt(attr[...], wo[rows[n], :])
 
-    for copy in staged[0]:
-        copy.wait()
+    kvo[0, :, :HD] = kin[:, their_cols(0)]
+    kvo[0, :, HD:] = vin[:, their_cols(0)]
     send_swap(START, 0)
-    for copy in kept_tiles[0]:
-        copy.wait()
+    kv[0, pl.ds(4 * T, T), :HD] = kin[:, mine_cols(0)]
+    kv[0, pl.ds(4 * T, T), HD:] = vin[:, mine_cols(0)]
     send_z(START, 0, 4)
-    for copy in staged[1]:
-        copy.wait()
+    kvo[1, :, :HD] = kin[:, their_cols(1)]
+    kvo[1, :, HD:] = vin[:, their_cols(1)]
     send_swap(START, 1)
     arrived(slot(0, 7), fr.at[0, 7])
     send_z(START, 0, 7)
     g_copy.wait()
     send_gathered(START, 0)
     send_own_x(START, 0)
-    for copy in kept_tiles[1]:
-        copy.wait()
+    kv[1, pl.ds(4 * T, T), :HD] = kin[:, mine_cols(1)]
+    kv[1, pl.ds(4 * T, T), HD:] = vin[:, mine_cols(1)]
     send_z(START, 1, 4)
-    for copy in staged[2]:
-        copy.wait()
+    kvo[2, :, :HD] = kin[:, their_cols(2)]
+    kvo[2, :, HD:] = vin[:, their_cols(2)]
     send_swap(START, 2)
     arrived(slot(1, 7), fr.at[1, 7])
     send_z(START, 1, 7)
@@ -443,7 +415,9 @@
     send_other_x(START, 0)
     forward(START, 0, 0, 1)
     forward(START, 0, 1, 0)
-    qo_copy.wait()
+    q_copy.wait()
+    qo[...] = qin[:, pl.ds(theirs, HALF)]
+    qb[0] = qin[:, pl.ds(mine, HALF)]
     send_queries(START)
     send_other_x(START, 1)
     send_own_x(START, 1)
@@ -462,15 +436,14 @@
     dop[...] = attn_grad(wo)
     send_attn_grad(START)
     dob[0] = attn_grad(wm)
-    for copy in kept_tiles[2]:
-        copy.wait()
+    kv[2, pl.ds(4 * T, T), :HD] = kin[:, mine_cols(2)]
+    kv[2, pl.ds(4 * T, T), HD:] = vin[:, mine_cols(2)]
     send_z(START, 2, 4)
     forward(START, 1, 1, 1)
     send_other_x(START, 2)
     send_own_x(START, 2)
     pass_on(START, 1)
     forward(START, 1, 0, 1)
-    q_copy.wait()
     arrived(qb.at[1], qr.at[0])
     attend(0)
     forward(START, 1, 1, 0)
@@ -489,28 +462,27 @@
     reduce_x(0, None)
     attend(2)
     pass_back(START, 1)
-    differentiate_values(2)
-    differentiate_keys(2)
+    differentiate(2, 0)
+    differentiate(2, 1)
     reduce_x(1, None)
     for h in range(NH):
         arrived(attr.at[:, cols(h)], atr.at[h])
     ms[0] = project(3).astype(BF)
     ms[1] = project(1).astype(BF)
     remote(START, ms, mr, mss.at[0], msr.at[0], sibling)
-    reduce_x(2, 1)
+    pass_back(START, 2)
     crossing_sum = project(2)
     arrived(mr, msr.at[0])
     ms2[...] = (crossing_sum + mr[0].astype(F32)).astype(BF)
     remote(START, ms2, mr2, mss.at[1], msr.at[1], across)
     kept = project(0) + mr[1].astype(F32)
-    reduce_x(2, 0)
+    reduce_x(2, None)
     reduce_z(0, None)
     reduce_z(1, None)
-    reduce_z(2, 1)
-    reduce_z(2, 0)
+    reduce_z(2, None)
     arrived(mr2, msr.at[1])
-    mo[...] = (kept + mr2[...].astype(F32)).astype(BF)
-    mixed_copy = local(mo, mixed, lsem.at[5])
+    res[0] = (kept + mr2[...].astype(F32)).astype(BF)
+    finals = [local(res.at[0], mixed, lsem.at[5])]
     send_z(WAIT, 0, 4)
     send_z(WAIT, 0, 7)
     send_z(WAIT, 1, 4)
@@ -518,6 +490,16 @@
     send_z(WAIT, 2, 4)
     send_z(WAIT, 2, 7)
 
+    for h in range(NH):
+        arrived(dql.at[:, cols(h)], dqr.at[h])
+        res[1, :, their_cols(h)] = dql[:, cols(h)]
+    finals.append(local(res.at[1], dq_out, lsem.at[6]))
+    for h in range(NH):
+        arrived(yr.at[h], byr.at[h])
+        res[2, :, their_cols(h)] = yr[h, :, :HD]
+        res[3, :, their_cols(h)] = yr[h, :, HD:]
+    finals.append(local(res.at[2], dk_out, lsem.at[7]))
+    finals.append(local(res.at[3], dv_out, lsem.at[8]))
     for n in range(3):
         send_gathered(WAIT, n)
     send_queries(WAIT)
@@ -526,21 +508,16 @@
     remote(WAIT, ms2, mr2, mss.at[1], msr.at[1], across)
     for h in range(NH):
         for send in (
-            send_swap, send_own_x, send_other_x, pass_on, pass_back, send_attended, send_query_grad,
+            send_swap, send_own_x, send_other_x, pass_on, pass_back, send_attended, send_query_grad, send_total,
         ):
             send(WAIT, h)
         for n in range(2):
             forward(WAIT, h, n, 0)
             forward(WAIT, h, n, 1)
-            for part in parts_of(h):
-                send_back(WAIT, h, n, part)
-        for part in parts_of(h):
-            send_reduced(WAIT, h, part)
-            send_total(WAIT, h, part)
-        arrived(dq_out.at[:, their_cols(h)], dqr.at[h])
-        arrived(dk_out.at[:, their_cols(h)], byr.at[h, 0])
-        arrived(dv_out.at[:, their_cols(h)], byr.at[h, 1])
-    mixed_copy.wait()
+            send_back(WAIT, h, n, None)
+        send_reduced(WAIT, h, None)
+    for copy in finals:
+        copy.wait()
 
 def hand_over(*refs):
     sources, results, held, ins, outs = refs[:4], refs[4:8], refs[8], refs[9], refs[10]
@@ -576,7 +553,8 @@
             pltpu.VMEM((4 * FULL, HALF), BF),
             pltpu.VMEM((2, T, HALF), BF),
             pltpu.VMEM((T, HALF), BF),
-            pltpu.VMEM((2, T, HALF), BF),
+            pltpu.VMEM((T, HALF), BF),
+            pltpu.VMEM((T, HALF), BF),
             pltpu.VMEM((2, T, WIN), BF),
             pltpu.VMEM((2, T, HD), F32),
             pltpu.VMEM((2, 1, WIN), F32),
@@ -585,25 +563,29 @@
             pltpu.VMEM((NH, 2 * SIDE, 2 * HD), F32),
             pltpu.VMEM((NH, 2, 2 * T, 2 * HD), BF),
             pltpu.VMEM((NH, 2, 2 * T, 2 * HD), BF),
-            pltpu.VMEM((NH, 2, T, 2 * HD), BF),
+            pltpu.VMEM((NH, T, 2 * HD), BF),
+            pltpu.VMEM((NH, T, 2 * HD), BF),
             pltpu.VMEM((2, T, FULL), BF),
             pltpu.VMEM((2, T, FULL), BF),
+            pltpu.VMEM((T, FULL), BF),
+            pltpu.VMEM((T, FULL), BF),
+            pltpu.VMEM((4, T, FULL), BF),
             pltpu.VMEM((T, FULL), BF),
             pltpu.VMEM((T, FULL), BF),
             pltpu.VMEM((T, FULL), BF),
             pltpu.VMEM((NH, T, 2 * HD), BF),
             pltpu.VMEM((NH, T, 2 * HD), BF),
             pltpu.VMEM((NH, T, 2 * HD), BF),
-            dma((6,)),
-            dma((NH, 4)),
+            dma((9,)),
+            dma((2,)),
             dma((NH, 14)),
             dma((NH, 12)),
             dma((NH, 2, 2, 3)),
             dma((NH, 2, 2, 3)),
             dma((NH, 2, 2)),
             dma((NH, 2, 2)),
-            dma((NH, 2)),
-            dma((NH, 2)),
+            dma((NH,)),
+            dma((NH,)),
             dma((3,)),
             dma((3,)),
             dma((2,)),

time: 78 us -> 80.5 us (1.032); the launches traced: 77.7 us -> 79.1 us
  Pallas kernels: 77.1 us -> 78.4 us
    pallas_call x1, Pallas kernels: 75 us -> 76.4 us  [on_device(): pl.pallas_call(kernel, out_shape=(block, block, block, block), in_specs=[...]
where the time goes in v8:
time: 80.5 us; the launch traced here: 79.1 us
  Pallas kernels  78.4 us (97%)
    pallas_call x1, Pallas kernels, on_device(): pl.pallas_call(kernel, out_shape=(block, block, block, block), in_specs=[...  76.4 us
    pallas_call x1, Pallas kernels, on_device(): pl.pallas_call(hand_over, out_shape=(block, block, block, block), in_spec...  2.07 us

profile of v8, /device:TPU:32, one launch (start us, length us, event | category | flops | bytes accessed | tf_op | source)
XLA Modules:
  0.0 79.1 jit_solution(7848308168385659082)
XLA Ops:
  0.6 76.4 %shard_map.93 = (bf16[160,768]{1,0:T(8,128)(2,1)}, bf16[160,768]{1,0:T(8,128)(2,1)}, bf16[160,768]{1,0:T(8,128)(2,1)}, bf16[160,768]{1,0:T(8,128)(2,1)}) custom-call(bf16[160,768]{1,0:T(8,128)(2,1)} %q_in.1, bf16[160,768]{1,0:T(8,128)(2,1)} %k_in.1, bf16[160,768]{1,0:T(8,128)(2,1)} %v_in.1, bf16[3072,768]{1,0:T(8,128)(2,1)} %w_in.1, bf16[160,768]{1,0:T(8,128)(2,1)} %g_in.1, ...), custom_call_target="tpu_custom_call" | custom-call | tf_op jit(solution)/shard_map/pallas_call | solution.py:539
  77.0 2.1 %shard_map.94 = (bf16[160,768]{1,0:T(8,128)(2,1)}, bf16[160,768]{1,0:T(8,128)(2,1)}, bf16[160,768]{1,0:T(8,128)(2,1)}, bf16[160,768]{1,0:T(8,128)(2,1)}) custom-call(bf16[160,768]{1,0:T(8,128)(2,1)} %get-tuple-element.8.refs_0_, bf16[160,768]{1,0:T(8,128)(2,1)} %get-tuple-element.9.refs_1_, bf16[160,768]{1,0:T(8,128)(2,1)} %get-tuple-element.10.refs_2_, ...), custom_call_target="tpu_custom_call" | custom-call | tf_op jit(solution)/shard_map/pallas_call | solution.py:608

commit v9 on v6

--- a/solution.py
+++ b/solution.py
@@ -395,6 +395,7 @@
     for copy in kept_tiles[0]:
         copy.wait()
     send_z(START, 0, 4)
+    send_own_x(START, 0)
     for copy in staged[1]:
         copy.wait()
     send_swap(START, 1)
@@ -402,81 +403,80 @@
     send_z(START, 0, 7)
     g_copy.wait()
     send_gathered(START, 0)
-    send_own_x(START, 0)
+    forward(START, 0, 0, 0)
+    send_other_x(START, 0)
     for copy in kept_tiles[1]:
         copy.wait()
     send_z(START, 1, 4)
-    for copy in staged[2]:
-        copy.wait()
-    send_swap(START, 2)
     arrived(slot(1, 7), fr.at[1, 7])
     send_z(START, 1, 7)
-    forward(START, 0, 0, 0)
-    send_other_x(START, 0)
     forward(START, 0, 0, 1)
-    forward(START, 0, 1, 0)
+    send_other_x(START, 1)
     qo_copy.wait()
     send_queries(START)
-    send_other_x(START, 1)
-    send_own_x(START, 1)
+    forward(START, 0, 1, 1)
     arrived(gall.at[2], gr.at[1])
     send_gathered(START, 2)
+    for copy in staged[2]:
+        copy.wait()
+    send_swap(START, 2)
+    forward(START, 0, 1, 0)
+    send_own_x(START, 1)
     send_gathered(START, 1)
-    forward(START, 0, 1, 1)
-    pass_on(START, 0)
-    arrived(slot(2, 7), fr.at[2, 7])
-    send_z(START, 2, 7)
-    forward(START, 1, 0, 0)
     for copy in w_copies:
         copy.wait()
     arrived(gall.at[1], gr.at[0])
     arrived(gall.at[3], gr.at[2])
     dop[...] = attn_grad(wo)
     send_attn_grad(START)
+    for copy in kept_tiles[2]:
+        copy.wait()
+    send_z(START, 2, 4)
     dob[0] = attn_grad(wm)
-    for copy in kept_tiles[2]:
-        copy.wait()
-    send_z(START, 2, 4)
-    forward(START, 1, 1, 1)
-    send_other_x(START, 2)
+    forward(START, 1, 1, 0)
+    forward(START, 1, 0, 0)
+    forward(START, 1, 0, 1)
     send_own_x(START, 2)
-    pass_on(START, 1)
-    forward(START, 1, 0, 1)
+    arrived(slot(2, 7), fr.at[2, 7])
+    send_z(START, 2, 7)
     q_copy.wait()
     arrived(qb.at[1], qr.at[0])
     attend(0)
-    forward(START, 1, 1, 0)
+    forward(START, 1, 1, 1)
+    pass_on(START, 1)
+    send_other_x(START, 2)
     arrived(dob.at[1], qr.at[1])
     differentiate(0, 0)
     differentiate(0, 1)
-    forward(START, 2, 1, 1)
     forward(START, 2, 1, 0)
-    forward(START, 2, 0, 0)
     attend(1)
     forward(START, 2, 0, 1)
+    pass_back(START, 2)
     pass_back(START, 0)
+    pass_on(START, 0)
+    forward(START, 2, 1, 1)
+    forward(START, 2, 0, 0)
     pass_on(START, 2)
     differentiate(1, 0)
     differentiate(1, 1)
     reduce_x(0)
+    pass_back(START, 1)
     attend(2)
-    pass_back(START, 1)
     differentiate(2, 0)
     differentiate(2, 1)
-    reduce_x(1)
     for h in range(NH):
         arrived(attr.at[:, cols(h)], atr.at[h])
     ms[0] = project(3).astype(BF)
     ms[1] = project(1).astype(BF)
     remote(START, ms, mr, mss.at[0], msr.at[0], sibling)
-    pass_back(START, 2)
+    reduce_x(1)
+    reduce_z(0)
     crossing_sum = project(2)
     arrived(mr, msr.at[0])
     ms2[...] = (crossing_sum + mr[0].astype(F32)).astype(BF)
     remote(START, ms2, mr2, mss.at[1], msr.at[1], across)
     kept = project(0) + mr[1].astype(F32)
     reduce_x(2)
-    reduce_z(0)
     reduce_z(1)
     reduce_z(2)
     arrived(mr2, msr.at[1])

time: 78.1 us -> 78.1 us (level)
  no operation moved by 1% of the time
where the time goes in v9:
time: 78.1 us; the launch traced here: 77.9 us
  Pallas kernels  77.2 us (99%)
    pallas_call x1, Pallas kernels, on_device(): pl.pallas_call(kernel, out_shape=(block, block, block, block), in_specs=[...  75.2 us
    pallas_call x1, Pallas kernels, on_device(): pl.pallas_call(hand_over, out_shape=(block, block, block, block), in_spec...  2.07 us

profile of v9, /device:TPU:32, one launch (start us, length us, event | category | flops | bytes accessed | tf_op | source)
XLA Modules:
  0.0 77.9 jit_solution(8623370114255456019)
XLA Ops:
  0.6 75.2 %shard_map.93 = (bf16[160,768]{1,0:T(8,128)(2,1)}, bf16[160,768]{1,0:T(8,128)(2,1)}, bf16[160,768]{1,0:T(8,128)(2,1)}, bf16[160,768]{1,0:T(8,128)(2,1)}) custom-call(bf16[160,768]{1,0:T(8,128)(2,1)} %q_in.1, bf16[160,768]{1,0:T(8,128)(2,1)} %k_in.1, bf16[160,768]{1,0:T(8,128)(2,1)} %v_in.1, bf16[3072,768]{1,0:T(8,128)(2,1)} %w_in.1, bf16[160,768]{1,0:T(8,128)(2,1)} %g_in.1, ...), custom_call_target="tpu_custom_call" | custom-call | tf_op jit(solution)/shard_map/pallas_call | solution.py:530
  75.8 2.1 %shard_map.94 = (bf16[160,768]{1,0:T(8,128)(2,1)}, bf16[160,768]{1,0:T(8,128)(2,1)}, bf16[160,768]{1,0:T(8,128)(2,1)}, bf16[160,768]{1,0:T(8,128)(2,1)}) custom-call(bf16[160,768]{1,0:T(8,128)(2,1)} %get-tuple-element.8.refs_0_, bf16[160,768]{1,0:T(8,128)(2,1)} %get-tuple-element.9.refs_1_, bf16[160,768]{1,0:T(8,128)(2,1)} %get-tuple-element.10.refs_2_, ...), custom_call_target="tpu_custom_call" | custom-call | tf_op jit(solution)/shard_map/pallas_call | solution.py:594

commit v10 on v6

--- a/solution.py
+++ b/solution.py
@@ -304,30 +304,31 @@
             att[a, :, cols(h)] = (total[:, :HD] * inverse).astype(BF)
         send_attended(START, h)
 
-    def differentiate(h, a):
-        q = qb[a, :, cols(h)]
-        do = dob[a, :, cols(h)].astype(F32)
-        window = pl.ds(a * SIDE, WIN)
-        k = kv[h, window, pl.ds(0, HD)]
-        weights = pb[a]
-        inverse = rb_sum[a]
-        row_dot = jnp.sum(do * att[a, :, cols(h)].astype(F32) * (inverse * scale), axis=1, keepdims=True)
-        do_sum = (do * inverse).astype(BF)
-        weight_grad = nt((do * (inverse * scale)).astype(BF), kv[h, window, pl.ds(HD, HD)])
-        score_grad = weights * (weight_grad - row_dot).astype(BF)
-        dqb[a, :, cols(h)] = nn(score_grad, k).astype(BF)
-        for part, lhs, rhs in ((0, score_grad, q), (1, weights, do_sum)):
-            grad = tn(lhs, rhs)
-            lane = pl.ds(part * HD, HD)
-            if a == 0:
-                xs[h, 1, :, lane] = grad[:SIDE].astype(BF)
-                acc[h, :, lane] = grad[SIDE:]
-            else:
-                acc[h, :, lane] += grad[:2 * SIDE]
-                xs[h, 0, :, lane] = grad[2 * SIDE:].astype(BF)
-        send_back(START, h, 1 - a)
-        if a == 1:
-            send_query_grad(START, h)
+    def differentiate(h):
+        for a in range(2):
+            q = qb[a, :, cols(h)]
+            do = dob[a, :, cols(h)].astype(F32)
+            window = pl.ds(a * SIDE, WIN)
+            k = kv[h, window, pl.ds(0, HD)]
+            weights = pb[a]
+            scaled = rb_sum[a] * scale
+            row_dot = jnp.sum(do * att[a, :, cols(h)].astype(F32) * scaled, axis=1, keepdims=True)
+            do_sum = (do * rb_sum[a]).astype(BF)
+            weight_grad = nt((do * scaled).astype(BF), kv[h, window, pl.ds(HD, HD)])
+            score_grad = weights * (weight_grad - row_dot).astype(BF)
+            dqb[a, :, cols(h)] = nn(score_grad, k).astype(BF)
+            for part, lhs, rhs in ((0, score_grad, q), (1, weights, do_sum)):
+                grad = tn(lhs, rhs)
+                lane = pl.ds(part * HD, HD)
+                if a == 0:
+                    xs[h, 1, :, lane] = grad[:SIDE].astype(BF)
+                    acc[h, :, lane] = grad[SIDE:]
+                else:
+                    acc[h, :, lane] += grad[:2 * SIDE]
+                    xs[h, 0, :, lane] = grad[2 * SIDE:].astype(BF)
+        send_back(START, h, 1)
+        send_back(START, h, 0)
+        send_query_grad(START, h)
 
     def reduce_x(h):
         for n, there, crossing in ((0, has_near, near_cross), (1, has_far, far_cross)):
@@ -447,8 +448,7 @@
     attend(0)
     forward(START, 1, 1, 0)
     arrived(dob.at[1], qr.at[1])
-    differentiate(0, 0)
-    differentiate(0, 1)
+    differentiate(0)
     forward(START, 2, 1, 1)
     forward(START, 2, 1, 0)
     forward(START, 2, 0, 0)
@@ -456,13 +456,11 @@
     forward(START, 2, 0, 1)
     pass_back(START, 0)
     pass_on(START, 2)
-    differentiate(1, 0)
-    differentiate(1, 1)
+    differentiate(1)
     reduce_x(0)
     attend(2)
     pass_back(START, 1)
-    differentiate(2, 0)
-    differentiate(2, 1)
+    differentiate(2)
     reduce_x(1)
     for h in range(NH):
         arrived(attr.at[:, cols(h)], atr.at[h])

time: 78.1 us -> 78.8 us (level)
  no operation moved by 1% of the time
where the time goes in v10:
time: 78.8 us; the launch traced here: 77.8 us
  Pallas kernels  77.2 us (98%)
    pallas_call x1, Pallas kernels, on_device(): pl.pallas_call(kernel, out_shape=(block, block, block, block), in_specs=[...  75.1 us
    pallas_call x1, Pallas kernels, on_device(): pl.pallas_call(hand_over, out_shape=(block, block, block, block), in_spec...  2.07 us

profile of v10, /device:TPU:32, one launch (start us, length us, event | category | flops | bytes accessed | tf_op | source)
XLA Modules:
  0.0 77.8 jit_solution(12761435895294230698)
XLA Ops:
  0.6 75.1 %shard_map.93 = (bf16[160,768]{1,0:T(8,128)(2,1)}, bf16[160,768]{1,0:T(8,128)(2,1)}, bf16[160,768]{1,0:T(8,128)(2,1)}, bf16[160,768]{1,0:T(8,128)(2,1)}) custom-call(bf16[160,768]{1,0:T(8,128)(2,1)} %q_in.1, bf16[160,768]{1,0:T(8,128)(2,1)} %k_in.1, bf16[160,768]{1,0:T(8,128)(2,1)} %v_in.1, bf16[3072,768]{1,0:T(8,128)(2,1)} %w_in.1, bf16[160,768]{1,0:T(8,128)(2,1)} %g_in.1, ...), custom_call_target="tpu_custom_call" | custom-call | tf_op jit(solution)/shard_map/pallas_call | solution.py:528
  75.7 2.1 %shard_map.94 = (bf16[160,768]{1,0:T(8,128)(2,1)}, bf16[160,768]{1,0:T(8,128)(2,1)}, bf16[160,768]{1,0:T(8,128)(2,1)}, bf16[160,768]{1,0:T(8,128)(2,1)}) custom-call(bf16[160,768]{1,0:T(8,128)(2,1)} %get-tuple-element.8.refs_0_, bf16[160,768]{1,0:T(8,128)(2,1)} %get-tuple-element.9.refs_1_, bf16[160,768]{1,0:T(8,128)(2,1)} %get-tuple-element.10.refs_2_, ...), custom_call_target="tpu_custom_call" | custom-call | tf_op jit(solution)/shard_map/pallas_call | solution.py:592

commit v11 on v6

--- a/solution.py
+++ b/solution.py
@@ -78,17 +78,25 @@
     theirs = pl.multiple_of((1 - p) * HALF, 128)
     scale = HD ** (-0.5)
 
+    spans = (
+        (pl.ds(0, SIDE), has_up & has_down),
+        (pl.ds(T, 2 * T), jnp.logical_not(has_down)),
+        (pl.ds(0, 2 * T), jnp.logical_not(has_up)),
+    )
+
     @pl.when(jnp.logical_not(has_down))
     def _():
         for s in (0, 3, 6, 9):
             kv[:, pl.ds(s * T, T), :] = jnp.zeros((NH, T, 2 * HD), BF)
         rz[:, 1] = jnp.zeros((NH, 2 * T, 2 * HD), BF)
+        rx[:, :, pl.ds(0, T), :] = jnp.zeros((NH, 2, T, 2 * HD), BF)
 
     @pl.when(jnp.logical_not(has_up))
     def _():
         for s in (2, 5, 8, 11):
             kv[:, pl.ds(s * T, T), :] = jnp.zeros((NH, T, 2 * HD), BF)
         rz[:, 0] = jnp.zeros((NH, 2 * T, 2 * HD), BF)
+        rx[:, :, pl.ds(2 * T, T), :] = jnp.zeros((NH, 2, T, 2 * HD), BF)
 
     for n, side, there, crossing in ((0, 0, has_near, near_cross), (1, 3, has_far, far_cross)):
         @pl.when(jnp.logical_not(there))
@@ -239,10 +247,11 @@
 
     def send_back(act, h, n):
         device, there, crossing = ((far, has_far, far_cross), (near, has_near, near_cross))[n]
-        remote(
-            act, xs.at[h, n], rx.at[h, n], bxs.at[h, n, 0], bxr.at[h, n, 0], device,
-            there & jnp.logical_not(crossing),
-        )
+        for rows, cond in spans:
+            remote(
+                act, xs.at[h, n, rows], rx.at[h, n, rows], bxs.at[h, n, 0], bxr.at[h, n, 0], device,
+                there & jnp.logical_not(crossing) & cond,
+            )
         middle = xs.at[h, n, pl.ds(T, T)]
         if h in DIRECT_BACK:
             remote(act, middle, rx.at[h, n, pl.ds(T, T)], bxs.at[h, n, 2], bxr.at[h, n, 1], device, crossing)
@@ -331,7 +340,8 @@
 
     def reduce_x(h):
         for n, there, crossing in ((0, has_near, near_cross), (1, has_far, far_cross)):
-            arrived(rx.at[h, n], bxr.at[h, n, 0], there & jnp.logical_not(crossing))
+            for rows, cond in spans:
+                arrived(rx.at[h, n, rows], bxr.at[h, n, 0], there & jnp.logical_not(crossing) & cond)
             arrived(rx.at[h, n, pl.ds(T, T)], bxr.at[h, n, 1], crossing)
             arrived(rx.at[h, n, pl.ds((1 - e) * T, T)], bxr.at[h, n, 2], crossing & has_back)
         for n in range(2):

time: 78.1 us -> 79.3 us (1.015)
  the two profiles are of different devices: /device:TPU:32 before, /device:TPU:22 now
where the time goes in v11:
time: 79.3 us; the launch traced here: 79.2 us
  Pallas kernels  78.5 us (99%)
    pallas_call x1, Pallas kernels, on_device(): pl.pallas_call(kernel, out_shape=(block, block, block, block), in_specs=[...  76.5 us
    pallas_call x1, Pallas kernels, on_device(): pl.pallas_call(hand_over, out_shape=(block, block, block, block), in_spec...  2.07 us

profile of v11, /device:TPU:22, one launch (start us, length us, event | category | flops | bytes accessed | tf_op | source)
XLA Modules:
  0.0 79.2 jit_solution(3465865850198952326)
XLA Ops:
  0.6 76.5 %shard_map.93 = (bf16[160,768]{1,0:T(8,128)(2,1)}, bf16[160,768]{1,0:T(8,128)(2,1)}, bf16[160,768]{1,0:T(8,128)(2,1)}, bf16[160,768]{1,0:T(8,128)(2,1)}) custom-call(bf16[160,768]{1,0:T(8,128)(2,1)} %q_in.1, bf16[160,768]{1,0:T(8,128)(2,1)} %k_in.1, bf16[160,768]{1,0:T(8,128)(2,1)} %v_in.1, bf16[3072,768]{1,0:T(8,128)(2,1)} %w_in.1, bf16[160,768]{1,0:T(8,128)(2,1)} %g_in.1, ...), custom_call_target="tpu_custom_call" | custom-call | tf_op jit(solution)/shard_map/pallas_call | solution.py:540
  77.1 2.1 %shard_map.94 = (bf16[160,768]{1,0:T(8,128)(2,1)}, bf16[160,768]{1,0:T(8,128)(2,1)}, bf16[160,768]{1,0:T(8,128)(2,1)}, bf16[160,768]{1,0:T(8,128)(2,1)}) custom-call(bf16[160,768]{1,0:T(8,128)(2,1)} %get-tuple-element.8.refs_0_, bf16[160,768]{1,0:T(8,128)(2,1)} %get-tuple-element.9.refs_1_, bf16[160,768]{1,0:T(8,128)(2,1)} %get-tuple-element.10.refs_2_, ...), custom_call_target="tpu_custom_call" | custom-call | tf_op jit(solution)/shard_map/pallas_call | solution.py:604
